TPU v7x, 128 devices: a whole 4x4x4 slice. The times are simulated.
128 devices in a mesh: layer: 8 (over x, core), feat: 16 (over y, z).
Axes of the slice: x: 4, y: 4, z: 4, core: 2. Of those that a mesh axis runs over, the one named last changes fastest.
Arguments:
- acts_in: bfloat16 [8, 256, 3584], P('layer', 'feat'), may hold values from -6 to 6
- targets: bfloat16 [8, 256, 3584], P('layer', 'feat'), may hold values from -6 to 6
- enc_weight: bfloat16 [128, 3584, 1536], P(('layer', 'feat')), may hold values from -0.09375 to 0.09375
- dec_weight: bfloat16 [128, 1536, 3584], P(('layer', 'feat')), may hold values from -0.0390625 to 0.0390625
- thresholds: float32 [128, 1536], P(('layer', 'feat')), may hold values from 0 to 0.5
- skip_weight: bfloat16 [8, 3584, 3584], P('layer', 'feat'), may hold values from -0.09375 to 0.09375
- dec_bias: float32 [8, 3584], P('layer'), may hold values from -3 to 3
- owner: int32 [128], replicated, may hold values from 0 to 7, as said below
Outputs:
- errors: bfloat16 [8, 256, 3584], P('layer', 'feat')
Inputs may be any that keep to these rules, and one draw needn't show every extreme that they name: `owner`: blocks are numbered group by group, 16 to a group; a block of group g belongs to layer g or a later one; at least half of each group's blocks belong to its own layer, and the last group's all do; some block of group 0 belongs to the last layer.
All inputs are finite; a program needn't handle non-finite values.
Results may differ from a plain program's by a relative error of at most 0.0059.
Values may be sent and summed in bfloat16 or wider, within the bound.
No kernel may reach another device: no remote copies, remote signals or barrier semaphores. Data moves between devices by JAX's collectives and lax.ppermute only.
A program may use at most 192 MiB of HBM per device.

v0:
```python
import jax
import jax.numpy as jnp
from jax import lax
from jax.sharding import PartitionSpec as P


def per_device(acts_in, targets, enc_weight, dec_weight, thresholds, skip_weight, dec_bias, owner):
    width = lax.axis_size("feat")
    group = lax.axis_index("layer")
    column = lax.axis_index("feat")
    mine = owner[group * width + column]
    whole = lax.all_gather(acts_in, "feat", axis=1, tiled=True)
    tokens = whole.shape[1]
    piece = lax.all_gather(whole, "layer", axis=0, tiled=True)
    layer_ids = jnp.arange(piece.shape[0], dtype=jnp.int32)
    hit = (layer_ids == mine)[:, None, None]
    lent = jnp.sum(jnp.where(hit, piece, jnp.zeros_like(piece)), axis=0)
    pre = jnp.dot(lent, enc_weight[0], preferred_element_type=jnp.float32) - thresholds[0][None, :]
    act = jnp.maximum(pre, 0.0).astype(jnp.bfloat16)
    partial_value = jnp.dot(act, dec_weight[0], preferred_element_type=jnp.float32)
    span = skip_weight.shape[1]
    columns = lax.dynamic_slice_in_dim(whole[0], column * span, span, 1)
    skipped = jnp.dot(columns, skip_weight[0], preferred_element_type=jnp.float32)
    shard = tokens // width
    row_ids = jnp.arange(lax.axis_size(("layer", "feat")) * shard, dtype=jnp.int32)
    layer_of = row_ids // tokens
    token_of = row_ids % tokens
    picked = jnp.take(partial_value, token_of, axis=0)
    picked_skip = jnp.take(skipped, token_of, axis=0)
    zeros = jnp.zeros_like(picked)
    own = jnp.where((layer_of == mine)[:, None], picked, zeros)
    home = jnp.where((layer_of == group)[:, None], picked_skip, zeros)
    recon = lax.psum_scatter(own + home, ("layer", "feat"), scatter_dimension=0, tiled=True)
    total = recon + dec_bias[0][None, :] - targets[0].astype(jnp.float32)
    return total.astype(jnp.bfloat16)[None]


def solution(mesh):
    placed = (
        P("layer", "feat", None),
        P("layer", "feat", None),
        P(("layer", "feat"), None, None),
        P(("layer", "feat"), None, None),
        P(("layer", "feat"), None),
        P("layer", "feat", None),
        P("layer", None),
        P(),
    )
    return jax.shard_map(
        per_device, mesh=mesh, in_specs=placed, out_specs=P("layer", "feat", None), check_vma=False
    )
```

profile of v0, /device:TPU:0, one launch (start us, length us, event | category | flops | bytes accessed | tf_op | source)
XLA Modules:
  0.0 914.3 jit_solution(17346621428369323367)
XLA Ops:
  6.5 0.0 copy-start
  6.5 0.0 all-gather.3.cloned.1.call-start
  6.5 0.7 all-gather.3.cloned.1.call-update
  7.3 0.0 all-gather.5.cloned.1.call-start
  7.3 49.5 %all-gather.3.cloned.1.call-done = bf16[1,256,3584]{2,1,0:T(8,128)(2,1)} async-done(((bf16[1,16,3584]{2,1,0:T(8,128)(2,1)}), bf16[1,256,3584]{2,1,0:T(8,128)(2,1)}) %all-gather.3.cloned.1.call-update) | async-done | bytes 1835024 | tf_op jit(solution)/shard_map/all_gather | solution.py:12
  56.8 0.0 all-gather.5.cloned.1.call-update
  56.9 0.0 reduce-scatter.2.cloned.1.call-start
  56.9 1.3 dynamic_slice.8
  58.2 0.7 reduce.1
  59.0 0.7 iota_compare_fusion
  59.7 0.6 compare_and_fusion
  60.2 1.3 fusion.31
  61.5 0.0 copy-done
  61.5 3.5 fusion.14
  65.1 27.6 %gather_fusion.1 = f32[2048,3584]{1,0:T(8,128)} fusion(f32[256,3584]{1,0:T(8,128)} %fusion.14, s32[2048]{0:T(1024)S(1)} %fusion.33), kind=kCustom, calls=%fused_computation.1.clone | custom fusion | bytes 58728448 | tf_op jit(solution)/shard_map/jit(_take)/gather | solution.py:29
  92.6 41.3 %all-gather.5.cloned.1.call-done = bf16[8,256,3584]{2,1,0:T(8,128)(2,1)} async-done(((bf16[1,256,3584]{2,1,0:T(8,128)(2,1)}), bf16[8,256,3584]{2,1,0:T(8,128)(2,1)}) %all-gather.5.cloned.1.call-update) | async-done | bytes 14680080 | tf_op jit(solution)/shard_map/all_gather | solution.py:14
  133.9 8.8 select_reduce_fusion
  142.8 14.9 %fusion.1 = f32[256,3584]{1,0:T(8,128)} fusion(bf16[1,1536,3584]{2,1,0:T(8,128)(2,1)} %param.13, bf16[256,3584]{1,0:T(8,128)(2,1)S(1)} %select_reduce_fusion, bf16[1,3584,1536]{2,1,0:T(8,128)(2,1)} %param.12, f32[1536]{0:T(1024)S(1)} %reduce.1), kind=kOutput, calls=%fused_computation.6 | convolution fusion | flops 5638324224 | bytes 27531264 | tf_op jit(solution)/shard_map/dot_general | solution.py:20
  157.6 0.0 copy-start.4
  157.6 0.0 copy-start.5
  157.6 0.0 copy-start.6
  157.6 27.3 %gather_fusion = f32[2048,3584]{1,0:T(8,128)} fusion(f32[256,3584]{1,0:T(8,128)} %fusion.1, s32[2048]{0:T(1024)S(1)} %fusion.33), kind=kCustom, calls=%fused_computation.clone | custom fusion | bytes 58728448 | tf_op jit(solution)/shard_map/jit(_take)/gather | solution.py:28
  184.9 0.0 copy-done.4
  184.9 0.0 copy-done.5
  184.9 0.0 copy-done.6
  184.9 31.0 %fusion = f32[2048,3584]{1,0:T(8,128)} fusion(f32[2048,3584]{1,0:T(8,128)} %gather_fusion.1, f32[2048,3584]{1,0:T(8,128)} %gather_fusion, pred[2048]{0:T(1024)(128)(4,1)S(1)} %copy-done.4, pred[2048]{0:T(1024)(128)(4,1)S(1)} %copy-done.5, pred[2048]{0:T(1024)(128)(4,1)S(1)} %copy-done.6), kind=kLoop, calls=%fused_computation.3 | loop fusion | flops 36700160 | bytes 88086528 | tf_op jit(solution)/shard_map/add | solution.py:33
  215.9 0.0 copy-start.1
  215.9 0.0 copy-start.3
  215.9 0.0 copy-start.2
  215.9 0.0 reduce-scatter.2.cloned.1.call-update
  215.9 0.8 copy-done.3
  216.8 689.4 %reduce-scatter.2.cloned.1.call-done = f32[16,3584]{1,0:T(8,128)} async-done(((f32[2048,3584]{1,0:T(8,128)}), f32[16,3584]{1,0:T(8,128)}) %reduce-scatter.2.cloned.1.call-update) | async-done | bytes 229392 | tf_op jit(solution)/shard_map/reduce_scatter | solution.py:33
  906.1 0.0 copy-done.2
  906.1 1.6 fusion.23
  907.8 0.0 copy-done.1
  (2 shorter events, 0.0 us)
Async XLA Ops:
  6.5 55.0 %copy-start = (bf16[1,224,3584]{2,1,0:T(8,128)(2,1)S(1)}, bf16[1,224,3584]{2,1,0:T(8,128)(2,1)}, u32[]{:S(2)}) copy-start(bf16[1,224,3584]{2,1,0:T(8,128)(2,1)} %param.15) | copy-start | bytes 4816900
  6.5 50.3 %all-gather.3.cloned.1.call-start = ((), (), s32[]{:S(2)}) async-start(), calls=%async_computation.1 | async-start | bytes 1949696 | tf_op jit(solution)/shard_map/all_gather | solution.py:12
  7.3 126.7 %all-gather.5.cloned.1.call-start = ((), (), s32[]{:S(2)}) async-start(), calls=%async_computation.2 | async-start | bytes 16515072 | tf_op jit(solution)/shard_map/all_gather | solution.py:14
  56.9 849.3 %reduce-scatter.2.cloned.1.call-start = ((), (), s32[]{:S(2)}) async-start(), calls=%async_computation.3 | async-start | bytes 29589504 | tf_op jit(solution)/shard_map/reduce_scatter | solution.py:33
  157.6 27.3 %copy-start.4 = (pred[2048]{0:T(1024)(128)(4,1)S(1)}, pred[2048]{0:T(1024)(128)(4,1)}, u32[]{:S(2)}) copy-start(pred[2048]{0:T(1024)(128)(4,1)} %compare_and_fusion) | copy-start | bytes 6148
  157.6 27.3 %copy-start.5 = (pred[2048]{0:T(1024)(128)(4,1)S(1)}, pred[2048]{0:T(1024)(128)(4,1)}, u32[]{:S(2)}) copy-start(pred[2048]{0:T(1024)(128)(4,1)} %get-tuple-element.6) | copy-start | bytes 6148
  157.6 27.3 %copy-start.6 = (pred[2048]{0:T(1024)(128)(4,1)S(1)}, pred[2048]{0:T(1024)(128)(4,1)}, u32[]{:S(2)}) copy-start(pred[2048]{0:T(1024)(128)(4,1)} %get-tuple-element.7) | copy-start | bytes 6148
  215.9 691.9 %copy-start.1 = (bf16[1,224,3584]{2,1,0:T(8,128)(2,1)S(1)}, bf16[1,224,3584]{2,1,0:T(8,128)(2,1)}, u32[]{:S(2)}) copy-start(bf16[1,224,3584]{2,1,0:T(8,128)(2,1)} %param.15) | copy-start | bytes 4816900
  215.9 0.8 copy-start.3
  215.9 690.3 %copy-start.2 = (bf16[1,16,3584]{2,1,0:T(8,128)(2,1)S(1)}, bf16[1,16,3584]{2,1,0:T(8,128)(2,1)}, u32[]{:S(2)}) copy-start(bf16[1,16,3584]{2,1,0:T(8,128)(2,1)} %param.11) | copy-start | bytes 344068
Sparse Core Ops, SparseCore 0:
  9.5 47.2 all-gather.2
  58.5 75.3 all-gather.4
  216.0 690.0 reduce-scatter.1
where the time goes:
time: 915 us; the launch traced here: 914 us
  waiting for transfers between devices  781 us (85%)
  local copies, waits for them, and re-layouts  57 us (6%)
  other arithmetic  44.8 us (5%)
  matrix products  18.4 us (2%)
  between operations  13.2 us (1%)
    reduce_scatter x1, waiting for transfers between devices, per_device(): lax.psum_scatter(own + home, ('layer', 'feat'), scatter_dimension=0, tile...  689 us
    all_gather x1, waiting for transfers between devices, per_device(): whole = lax.all_gather(acts_in, 'feat', axis=1, tiled=True)  49.5 us
    all_gather x1, waiting for transfers between devices, per_device(): piece = lax.all_gather(whole, 'layer', axis=0, tiled=True)  41.3 us
    add x1, other arithmetic, per_device(): own + home  31 us
    gather x1, local copies, waits for them, and re-layouts, per_device(): picked_skip = jnp.take(skipped, token_of, axis=0)  27.6 us
    gather x1, local copies, waits for them, and re-layouts, per_device(): picked = jnp.take(partial_value, token_of, axis=0)  27.3 us
  transfers between devices with their start and end apart: 3, of which 3 were waited for; matrix products, arithmetic and copies ran while one was open for 4% of the time, Pallas kernels for 0%

commit v1 on v0

v1 whole, which is shorter than its diff:
```python
import jax
import jax.numpy as jnp
from jax import lax
from jax.experimental import pallas as pl
from jax.experimental.pallas import tpu as pltpu
from jax.sharding import PartitionSpec as P

BF = jnp.bfloat16
F32 = jnp.float32


def pick_rows(source, index):
    count, (_, rows, width) = index.shape[0], source.shape

    def kernel(index_ref, source_ref, out_ref, sem):
        copies = [
            pltpu.make_async_copy(source_ref.at[index_ref[n]], out_ref.at[n], sem.at[n]) for n in range(count)
        ]
        for copy in copies:
            copy.start()
        for copy in copies:
            copy.wait()

    return pl.pallas_call(
        kernel,
        out_shape=jax.ShapeDtypeStruct((count, rows, width), source.dtype),
        in_specs=[pl.BlockSpec(memory_space=pltpu.SMEM), pl.BlockSpec(memory_space=pl.ANY)],
        out_specs=pl.BlockSpec(memory_space=pl.ANY),
        scratch_shapes=[pltpu.SemaphoreType.DMA((count,))],
        cost_estimate=pl.CostEstimate(flops=0, bytes_accessed=2 * count * rows * width * 2, transcendentals=0),
    )(index, source)


def sum_by_owner(parts, index, slots):
    count, rows, width = parts.shape
    step = width // 4

    def kernel(index_ref, parts_ref, out_ref, total):
        total[...] = jnp.zeros_like(total)
        for n in range(count):
            slot = index_ref[n]
            total[slot] = total[slot] + parts_ref[n].astype(F32)
        out_ref[...] = total[...].astype(out_ref.dtype)

    return pl.pallas_call(
        kernel,
        grid=(width // step,),
        out_shape=jax.ShapeDtypeStruct((slots, rows, width), BF),
        in_specs=[
            pl.BlockSpec(memory_space=pltpu.SMEM),
            pl.BlockSpec((count, rows, step), lambda i: (0, 0, i)),
        ],
        out_specs=pl.BlockSpec((slots, rows, step), lambda i: (0, 0, i)),
        scratch_shapes=[pltpu.VMEM((slots, rows, step), F32)],
        cost_estimate=pl.CostEstimate(flops=count * rows * width, bytes_accessed=(count + slots) * rows * width * 2, transcendentals=0),
    )(index, parts)


def per_device(acts_in, targets, enc_weight, dec_weight, thresholds, skip_weight, dec_bias, owner):
    width = lax.axis_size("feat")
    layers = lax.axis_size("layer")
    group = lax.axis_index("layer")
    shard, depth = acts_in.shape[1:]
    tokens = shard * width
    span = skip_weight.shape[1]
    mine = lax.dynamic_slice_in_dim(owner, group * width, width)

    cut = acts_in[0].reshape(shard, width, span).transpose(1, 0, 2)
    columns = lax.all_to_all(cut, "feat", 0, 0).reshape(tokens, span)
    skipped = jnp.dot(columns, skip_weight[0], preferred_element_type=F32)
    skip_sum = lax.psum_scatter(skipped, "feat", scatter_dimension=0, tiled=True)

    shards = lax.all_gather(acts_in[0], "layer", axis=0)
    sent = pick_rows(shards, mine)
    rows = lax.all_to_all(sent, "feat", 0, 0).reshape(tokens, depth)

    pre = jnp.dot(rows, enc_weight[0], preferred_element_type=F32) - thresholds[0][None, :]
    act = jnp.maximum(pre, 0.0).astype(BF)
    part = jnp.dot(act, dec_weight[0], preferred_element_type=F32).astype(BF)

    back = lax.all_to_all(part.reshape(width, shard, depth), "feat", 0, 0)
    slots = sum_by_owner(back, mine, layers)
    home = lax.all_to_all(slots, "layer", 0, 0)
    recon = jnp.sum(home.astype(F32), axis=0) + skip_sum
    total = recon + dec_bias[0][None, :] - targets[0].astype(F32)
    return total.astype(BF)[None]


def solution(mesh):
    placed = (
        P("layer", "feat", None),
        P("layer", "feat", None),
        P(("layer", "feat"), None, None),
        P(("layer", "feat"), None, None),
        P(("layer", "feat"), None),
        P("layer", "feat", None),
        P("layer", None),
        P(),
    )
    return jax.shard_map(
        per_device, mesh=mesh, in_specs=placed, out_specs=P("layer", "feat", None), check_vma=False
    )
```

time: 915 us -> 208 us (0.23)
  waiting for transfers between devices: 781 us -> 42.2 us
  Pallas kernels: 0 us -> 61.4 us
  blocking collectives: 0 us -> 60.9 us
  local copies, waits for them, and re-layouts: 57 us -> 2.49 us
  other arithmetic: 44.8 us -> 1.83 us
    reduce_scatter x1, waiting for transfers between devices: 689 us -> 0.02 us  [per_device(): lax.psum_scatter(skipped, 'feat', scatter_dimension=0, tiled=True)]
    all_gather x2 -> x0, waiting for transfers between devices: 90.8 us -> none  [the longest x1 49.5 us: per_device(): whole = lax.all_gather(acts_in, 'feat', axis=1, tiled=True)]
    pallas_call x0 -> x2, Pallas kernels: none -> 61.4 us  [the longest x1 57.5 us: pick_rows(): pl.pallas_call(kernel, out_shape=jax.ShapeDtypeStruct((count, rows, width...]
    gather x2 -> x0, local copies, waits for them, and re-layouts: 54.8 us -> none  [the longest x1 27.6 us: per_device(): picked_skip = jnp.take(skipped, token_of, axis=0)]
    all_to_all x0 -> x2, blocking collectives: none -> 46 us  [the longest x1 30.2 us: per_device(): back = lax.all_to_all(part.reshape(width, shard, depth), 'feat', 0, 0)]
    all_to_all x0 -> x2, waiting for transfers between devices: none -> 42.2 us  [the longest x1 27.7 us: per_device(): rows = lax.all_to_all(sent, 'feat', 0, 0).reshape(tokens, depth)]
    add x1 -> x0, other arithmetic: 31 us -> none  [per_device(): own + home]
    all_gather x0 -> x1, blocking collectives: none -> 14.9 us  [per_device(): shards = lax.all_gather(acts_in[0], 'layer', axis=0)]
  transfers between devices with their start and end apart: 3 -> 3, of which waited for: 3 -> 2; matrix products, arithmetic and copies ran while one was open for 4% -> 7% of each run, Pallas kernels for 0% -> 30%
where the time goes in v1:
time: 208 us; the launch traced here: 207 us
  Pallas kernels  61.4 us (30%)
  blocking collectives  60.9 us (29%)
  waiting for transfers between devices  42.2 us (20%)
  matrix products  16.8 us (8%)
  between operations  13.5 us (6%)
  starting transfers between devices  7.54 us (4%)
  local copies, waits for them, and re-layouts  2.49 us (1%)
    pallas_call x1, Pallas kernels, pick_rows(): pl.pallas_call(kernel, out_shape=jax.ShapeDtypeStruct((count, rows, width...  57.5 us
    all_to_all x1, blocking collectives, per_device(): back = lax.all_to_all(part.reshape(width, shard, depth), 'feat', 0, 0)  30.2 us
    all_to_all x1, waiting for transfers between devices, per_device(): rows = lax.all_to_all(sent, 'feat', 0, 0).reshape(tokens, depth)  27.7 us
    all_to_all x1, blocking collectives, per_device(): columns = lax.all_to_all(cut, 'feat', 0, 0).reshape(tokens, span)  15.8 us
    all_gather x1, blocking collectives, per_device(): shards = lax.all_gather(acts_in[0], 'layer', axis=0)  14.9 us
    all_to_all x1, waiting for transfers between devices, per_device(): home = lax.all_to_all(slots, 'layer', 0, 0)  14.5 us
    dot_general x1, matrix products, per_device(): part = jnp.dot(act, dec_weight[0], preferred_element_type=F32).astype(BF)  14.4 us
  transfers between devices with their start and end apart: 3, of which 2 were waited for; matrix products, arithmetic and copies ran while one was open for 7% of the time, Pallas kernels for 30%

profile of v1, /device:TPU:0, one launch (start us, length us, event | category | flops | bytes accessed | tf_op | source)
XLA Modules:
  0.0 206.7 jit_solution(16424082939207345040)
XLA Ops:
  6.5 0.0 copy-start
  6.5 0.0 reduce-scatter.2.cloned.1.call-start
  6.5 1.2 reshape_squeeze.3
  7.8 15.8 %all_to_all.20 = bf16[16,16,224]{2,1,0:T(8,128)(2,1)S(1)} all-to-all(bf16[16,16,224]{2,1,0:T(8,128)(2,1)S(1)} %bitcast.34), channel_id=1, replica_groups=mesh['layer'=8,'feat'=16] {'feat'}, dimensions={0} | all-to-all | bytes 229376 | tf_op jit(solution)/shard_map/all_to_all | solution.py:69
  23.6 0.0 copy-done
  23.6 2.4 %fusion.16 = f32[256,3584]{1,0:T(8,128)} fusion(bf16[256,224]{1,0:T(8,128)(2,1)S(1)} %bitcast.35, bf16[1,224,3584]{2,1,0:T(8,128)(2,1)S(1)} %copy-done), kind=kOutput, calls=%fused_computation.9 | convolution fusion | flops 411041792 | bytes 5390336 | tf_op jit(solution)/shard_map/dot_general | solution.py:70
  26.0 0.0 copy-start.5
  26.0 0.0 copy-start.1
  26.0 0.0 reduce-scatter.2.cloned.1.call-update
  26.0 0.6 copy-done.5
  26.7 0.6 dynamic_slice.3.index_ref
  27.3 0.0 copy-done.1
  27.3 14.9 %all_gather.3.source_ref = bf16[8,16,3584]{2,1,0:T(8,128)(2,1)} all-gather(bf16[1,16,3584]{2,1,0:T(8,128)(2,1)S(1)} %copy-done.1), channel_id=1, replica_groups=mesh['layer'=8,'feat'=16] {'layer'}, dimensions={0}, use_global_device_ids=true | all-gather | bytes 1032192 | tf_op jit(solution)/shard_map/all_gather | solution.py:73
  42.2 57.5 %shard_map.82 = bf16[16,16,3584]{2,1,0:T(8,128)(2,1)} custom-call(s32[16]{0:T(128)} %dynamic_slice.3.index_ref, bf16[8,16,3584]{2,1,0:T(8,128)(2,1)} %all_gather.3.source_ref), custom_call_target="tpu_custom_call" | custom-call | bytes 3670016 | tf_op jit(solution)/shard_map/pallas_call | solution.py:24
  99.7 0.0 copy-start.4
  99.7 3.7 %all-to-all-start = ((bf16[16,16,3584]{2,1,0:T(8,128)(2,1)}), bf16[16,16,3584]{2,1,0:T(8,128)(2,1)S(1)}, u32[]{:S(2)}, u32[]{:S(2)}) async-start(bf16[16,16,3584]{2,1,0:T(8,128)(2,1)} %shard_map.82), calls=%async_computation | async-start | bytes 3670016 | tf_op jit(solution)/shard_map/all_to_all | solution.py:75
  103.4 0.0 copy-done.4
  103.5 27.7 %all-to-all-done = bf16[16,16,3584]{2,1,0:T(8,128)(2,1)S(1)} async-done(((bf16[16,16,3584]{2,1,0:T(8,128)(2,1)}), bf16[16,16,3584]{2,1,0:T(8,128)(2,1)S(1)}, u32[]{:S(2)}, u32[]{:S(2)}) %all-to-all-start) | async-done | bytes 1835040 | tf_op jit(solution)/shard_map/all_to_all | solution.py:75
  131.1 14.4 %fusion.4 = bf16[256,3584]{1,0:T(8,128)(2,1)} fusion(bf16[1,1536,3584]{2,1,0:T(8,128)(2,1)} %param.11, bf16[256,3584]{1,0:T(8,128)(2,1)S(1)} %bitcast.32, bf16[1,3584,1536]{2,1,0:T(8,128)(2,1)} %param.10, f32[1536]{0:T(1024)S(1)} %reduce), kind=kOutput, calls=%fused_computation.4 | convolution fusion | flops 5639241728 | bytes 25696256 | tf_op jit(solution)/shard_map/dot_general | solution.py:79
  145.5 30.2 %all_to_all.21.parts_ref = bf16[16,16,3584]{2,1,0:T(8,128)(2,1)} all-to-all(bf16[16,16,3584]{2,1,0:T(8,128)(2,1)} %bitcast.33), channel_id=1, replica_groups=mesh['layer'=8,'feat'=16] {'feat'}, dimensions={0} | all-to-all | bytes 3670016 | tf_op jit(solution)/shard_map/all_to_all | solution.py:81
  175.7 0.0 copy-start.3
  175.7 3.9 %shard_map.83 = bf16[8,16,3584]{2,1,0:T(8,128)(2,1)} custom-call(s32[16]{0:T(128)} %dynamic_slice.3.index_ref, bf16[16,16,3584]{2,1,0:T(8,128)(2,1)} %all_to_all.21.parts_ref), custom_call_target="tpu_custom_call" | custom-call | flops 917504 | bytes 2752512 | tf_op jit(solution)/shard_map/pallas_call | solution.py:45
  179.7 0.0 copy-start.2
  179.7 3.8 %all-to-all-start.2 = ((bf16[8,16,3584]{2,1,0:T(8,128)(2,1)}), bf16[8,16,3584]{2,1,0:T(8,128)(2,1)S(1)}, u32[]{:S(2)}, u32[]{:S(2)}) async-start(bf16[8,16,3584]{2,1,0:T(8,128)(2,1)} %shard_map.83), calls=%async_computation.2 | async-start | bytes 1835008 | tf_op jit(solution)/shard_map/all_to_all | solution.py:83
  183.5 0.0 copy-done.3
  183.5 14.5 %all-to-all-done.2 = bf16[8,16,3584]{2,1,0:T(8,128)(2,1)S(1)} async-done(((bf16[8,16,3584]{2,1,0:T(8,128)(2,1)}), bf16[8,16,3584]{2,1,0:T(8,128)(2,1)S(1)}, u32[]{:S(2)}, u32[]{:S(2)}) %all-to-all-start.2) | async-done | bytes 917536 | tf_op jit(solution)/shard_map/all_to_all | solution.py:83
  198.0 0.1 convert_reduce_fusion
  198.2 0.0 reduce-scatter.2.cloned.1.call-done
  198.2 0.0 copy-done.2
  198.2 1.6 fusion.21
  (3 shorter events, 0.1 us)
Async XLA Ops:
  6.5 17.1 %copy-start = (bf16[1,224,3584]{2,1,0:T(8,128)(2,1)S(1)}, bf16[1,224,3584]{2,1,0:T(8,128)(2,1)}, u32[]{:S(2)}) copy-start(bf16[1,224,3584]{2,1,0:T(8,128)(2,1)} %param.13) | copy-start | bytes 4816900
  6.5 191.7 %reduce-scatter.2.cloned.1.call-start = ((), (), s32[]{:S(2)}) async-start(), calls=%async_computation.5 | async-start | bytes 3899392 | tf_op jit(solution)/shard_map/reduce_scatter | solution.py:71
  26.0 0.7 copy-start.5
  26.0 1.2 copy-start.1
  99.7 3.7 %copy-start.4 = (f32[1,1536]{1,0:T(1,128)S(1)}, f32[1,1536]{1,0:T(1,128)}, u32[]{:S(2)}) copy-start(f32[1,1536]{1,0:T(1,128)} %param.12) | copy-start | bytes 18436
  99.7 31.4 %all-to-all-start = ((bf16[16,16,3584]{2,1,0:T(8,128)(2,1)}), bf16[16,16,3584]{2,1,0:T(8,128)(2,1)S(1)}, u32[]{:S(2)}, u32[]{:S(2)}) async-start(bf16[16,16,3584]{2,1,0:T(8,128)(2,1)} %shard_map.82), calls=%async_computation | async-start | bytes 3670016 | tf_op jit(solution)/shard_map/all_to_all | solution.py:75
  175.7 7.8 %copy-start.3 = (f32[1,3584]{1,0:T(1,128)S(1)}, f32[1,3584]{1,0:T(1,128)}, u32[]{:S(2)}) copy-start(f32[1,3584]{1,0:T(1,128)} %param.14) | copy-start | bytes 43012
  179.7 18.6 %copy-start.2 = (bf16[1,16,3584]{2,1,0:T(8,128)(2,1)S(1)}, bf16[1,16,3584]{2,1,0:T(8,128)(2,1)}, u32[]{:S(2)}) copy-start(bf16[1,16,3584]{2,1,0:T(8,128)(2,1)} %param.9) | copy-start | bytes 344068
  179.7 18.4 %all-to-all-start.2 = ((bf16[8,16,3584]{2,1,0:T(8,128)(2,1)}), bf16[8,16,3584]{2,1,0:T(8,128)(2,1)S(1)}, u32[]{:S(2)}, u32[]{:S(2)}) async-start(bf16[8,16,3584]{2,1,0:T(8,128)(2,1)} %shard_map.83), calls=%async_computation.2 | async-start | bytes 1835008 | tf_op jit(solution)/shard_map/all_to_all | solution.py:83
Sparse Core Ops, SparseCore 0:
  26.2 74.4 reduce-scatter.1

commit v2 on v1

v2 whole, which is shorter than its diff:
```python
import functools

import jax
import jax.numpy as jnp
from jax import lax
from jax.experimental import pallas as pl
from jax.experimental.pallas import tpu as pltpu
from jax.sharding import PartitionSpec as P

BF = jnp.bfloat16
F32 = jnp.float32
MIB = 1 << 20
VMEM_LIMIT = 40 * MIB
WEIGHTS_LIMIT = 56 * MIB


def whole(memory_space):
    return pl.BlockSpec(memory_space=memory_space)


def pick_rows(near, far, place, cut):
    count, span = cut.shape[0], cut.shape[2]
    slots, rows, depth = near.shape
    padded = depth + -(-span // 128) * 128

    def kernel(place_ref, near_ref, far_ref, cut_ref, out_ref):
        for n in range(count):
            slot = place_ref[n]

            @pl.when(slot < slots)
            def _():
                out_ref[n, :, :depth] = near_ref[slot]

            @pl.when(slot >= slots)
            def _():
                out_ref[n, :, :depth] = far_ref[slot - slots]

            out_ref[n, :, depth : depth + span] = cut_ref[n]
            if padded > depth + span:
                out_ref[n, :, depth + span :] = jnp.zeros((rows, padded - depth - span), out_ref.dtype)

    return pl.pallas_call(
        kernel,
        out_shape=jax.ShapeDtypeStruct((count, rows, padded), near.dtype),
        in_specs=[whole(pltpu.SMEM)] + [whole(pltpu.VMEM)] * 3,
        out_specs=whole(pltpu.VMEM),
        compiler_params=pltpu.CompilerParams(vmem_limit_bytes=VMEM_LIMIT),
        cost_estimate=pl.CostEstimate(flops=0, bytes_accessed=2 * count * rows * padded * 2, transcendentals=0),
    )(place, near, far, cut)


def sum_by_place(parts, place, slots, after):
    count, rows, width = parts.shape
    step = 512

    def kernel(place_ref, parts_ref, after_ref, near_ref, far_ref, total):
        total[...] = jnp.zeros_like(total)
        for n in range(count):
            slot = place_ref[n]
            total[slot] = total[slot] + parts_ref[n].astype(F32)
        near_ref[...] = total[:slots].astype(BF)
        far_ref[...] = total[slots:].astype(BF)

    block = pl.BlockSpec((slots, rows, step), lambda i: (0, 0, i))
    return pl.pallas_call(
        kernel,
        grid=(width // step,),
        out_shape=[jax.ShapeDtypeStruct((slots, rows, width), BF)] * 2,
        in_specs=[whole(pltpu.SMEM), pl.BlockSpec((count, rows, step), lambda i: (0, 0, i)), whole(pl.ANY)],
        out_specs=[block, block],
        scratch_shapes=[pltpu.VMEM((2 * slots, rows, step), F32)],
        compiler_params=pltpu.CompilerParams(vmem_limit_bytes=VMEM_LIMIT),
        cost_estimate=pl.CostEstimate(flops=count * rows * width, bytes_accessed=(count + 2 * slots) * rows * width * 2, transcendentals=0),
    )(place, parts, after)


def encode_decode(x, enc, thresholds, dec, width, after):
    tokens, depth = x.shape[0], enc.shape[1]
    features = enc.shape[2]
    enc_cut, dec_cut = 512, 896
    enc_turns, dec_turns = features // enc_cut, width // dec_cut

    def kernel(x_ref, enc_ref, thr_ref, dec_ref, after_ref, act_ref, part_ref, enc_buf, dec_buf, enc_sem, dec_sem):
        def fetch_enc(n):
            at = pl.ds(n * enc_cut, enc_cut)
            return pltpu.make_async_copy(enc_ref.at[0, :, at], enc_buf.at[n], enc_sem.at[n])

        def fetch_dec(n):
            at = pl.ds(n * dec_cut, dec_cut)
            return pltpu.make_async_copy(dec_ref.at[0, :, at], dec_buf.at[n], dec_sem.at[n])

        for n in range(enc_turns):
            fetch_enc(n).start()
        for n in range(dec_turns):
            fetch_dec(n).start()
        for n in range(enc_turns):
            fetch_enc(n).wait()
            at = slice(n * enc_cut, (n + 1) * enc_cut)
            pre = jnp.dot(x_ref[:, :depth], enc_buf[n], preferred_element_type=F32) - thr_ref[:, at]
            act_ref[:, at] = jnp.maximum(pre, 0.0).astype(BF)
        for n in range(dec_turns):
            fetch_dec(n).wait()
            at = slice(n * dec_cut, (n + 1) * dec_cut)
            part_ref[:, at] = jnp.dot(act_ref[...], dec_buf[n], preferred_element_type=F32).astype(BF)

    return pl.pallas_call(
        kernel,
        out_shape=[jax.ShapeDtypeStruct((tokens, features), BF), jax.ShapeDtypeStruct((tokens, width), BF)],
        in_specs=[whole(pltpu.VMEM), whole(pl.ANY), whole(pltpu.VMEM), whole(pl.ANY), whole(pl.ANY)],
        out_specs=[whole(pltpu.VMEM)] * 2,
        scratch_shapes=[
            pltpu.VMEM((enc_turns, depth, enc_cut), BF),
            pltpu.VMEM((dec_turns, features, dec_cut), BF),
            pltpu.SemaphoreType.DMA((enc_turns,)),
            pltpu.SemaphoreType.DMA((dec_turns,)),
        ],
        compiler_params=pltpu.CompilerParams(vmem_limit_bytes=WEIGHTS_LIMIT),
        cost_estimate=pl.CostEstimate(flops=2 * tokens * features * (depth + width), bytes_accessed=features * (depth + width) * 2, transcendentals=0),
    )(x, enc, thresholds, dec, after)


def decode_rest(act, dec, begin, after):
    tokens, features = act.shape
    width = dec.shape[2] - begin
    cut = width // 2
    turns = width // cut

    def kernel(act_ref, dec_ref, after_ref, part_ref, dec_buf, dec_sem):
        def fetch(n):
            at = pl.ds(begin + n * cut, cut)
            return pltpu.make_async_copy(dec_ref.at[0, :, at], dec_buf.at[n], dec_sem.at[n])

        for n in range(turns):
            fetch(n).start()
        for n in range(turns):
            fetch(n).wait()
            at = slice(n * cut, (n + 1) * cut)
            part_ref[:, at] = jnp.dot(act_ref[...], dec_buf[n], preferred_element_type=F32).astype(BF)

    return pl.pallas_call(
        kernel,
        out_shape=jax.ShapeDtypeStruct((tokens, width), BF),
        in_specs=[whole(pltpu.VMEM), whole(pl.ANY), whole(pl.ANY)],
        out_specs=whole(pltpu.VMEM),
        scratch_shapes=[pltpu.VMEM((turns, features, cut), BF), pltpu.SemaphoreType.DMA((turns,))],
        compiler_params=pltpu.CompilerParams(vmem_limit_bytes=WEIGHTS_LIMIT),
        cost_estimate=pl.CostEstimate(flops=2 * tokens * features * width, bytes_accessed=features * width * 2, transcendentals=0),
    )(act, dec, after)


PIECES = 1


def per_device(chips, across, down, acts_in, targets, enc_weight, dec_weight, thresholds, skip_weight, dec_bias, owner):
    layers, width = 2 * chips, across * down
    group = lax.axis_index("layer")
    chip, core = group // 2, group % 2
    shard, depth = acts_in.shape[1:]
    tokens = shard * width
    span = skip_weight.shape[1]
    mine = lax.dynamic_slice_in_dim(owner, group * width, width)
    place = mine // 2 - chip + chips * (mine % 2 != core).astype(jnp.int32)
    swap = [(i, i ^ 1) for i in range(layers)]

    cut = acts_in[0].reshape(shard, width, span).transpose(1, 0, 2)

    later = [
        lax.ppermute(acts_in[0], "layer", [(i, i - 2 * s) for i in range(2 * s, layers)]) for s in range(1, chips)
    ]
    near = jnp.stack([acts_in[0], *later])
    far = lax.ppermute(near, "layer", swap)
    sent = pick_rows(near, far, place, cut)
    rows = lax.all_to_all(sent, "feat", 0, 0).reshape(tokens, sent.shape[2])
    skipped = jnp.dot(rows[:, depth : depth + span], skip_weight[0], preferred_element_type=F32).astype(BF)
    by_across = [[y * down + z for y in range(across)] for z in range(down)]
    by_down = [[y * down + z for z in range(down)] for y in range(across)]
    halfway = lax.psum_scatter(skipped, "feat", scatter_dimension=0, axis_index_groups=by_across, tiled=True)

    act, part = encode_decode(rows, enc_weight, thresholds, dec_weight, depth // PIECES, skipped)
    skip_sum = lax.psum_scatter(halfway.astype(F32), "feat", scatter_dimension=0, axis_index_groups=by_down, tiled=True)
    parts = [part]
    if PIECES == 2:
        parts.append(decode_rest(act, dec_weight, depth // PIECES, halfway))

    backs = [lax.all_to_all(part.reshape(width, shard, depth // PIECES), "feat", 0, 0) for part in parts]
    outs = []
    for back in backs:
        kept, given = sum_by_place(back, place, chips, outs[-1] if outs else halfway)
        taken = lax.ppermute(given, "layer", swap)
        pair = (kept.astype(F32) + taken.astype(F32)).astype(BF)
        arrived = [
            lax.ppermute(pair[s], "layer", [(i, i + 2 * s) for i in range(layers - 2 * s)]) for s in range(1, chips)
        ]
        outs.append(sum((a.astype(F32) for a in arrived), pair[0].astype(F32)))
    recon = jnp.concatenate(outs, axis=1) + skip_sum
    total = recon + dec_bias[0][None, :] - targets[0].astype(F32)
    return total.astype(BF)[None]


def solution(mesh):
    placed = (
        P("layer", "feat", None),
        P("layer", "feat", None),
        P(("layer", "feat"), None, None),
        P(("layer", "feat"), None, None),
        P(("layer", "feat"), None),
        P("layer", "feat", None),
        P("layer", None),
        P(),
    )
    chips, across = mesh.shape["layer"] // 2, 4
    down = mesh.shape["feat"] // across
    return jax.shard_map(
        functools.partial(per_device, chips, across, down),
        mesh=mesh,
        in_specs=placed,
        out_specs=P("layer", "feat", None),
        check_vma=False,
    )
```

time: 208 us -> 143 us (0.69)
  Pallas kernels: 61.4 us -> 19.3 us
  waiting for transfers between devices: 42.2 us -> 20.9 us
  matrix products: 16.8 us -> 1.85 us
  starting transfers between devices: 7.54 us -> 13.5 us
  blocking collectives: 60.9 us -> 64.6 us
  other arithmetic: 1.83 us -> 4.51 us
    all_to_all x2 -> x0, waiting for transfers between devices: 42.2 us -> none  [the longest x1 27.7 us: per_device(): rows = lax.all_to_all(sent, 'feat', 0, 0).reshape(tokens, depth)]
    pallas_call x2 -> x3, Pallas kernels: 61.4 us -> 19.3 us  [the longest x1 14.9 us: encode_decode(): pl.pallas_call(kernel, out_shape=[jax.ShapeDtypeStruct((tokens, features)...]
    all_to_all x2, blocking collectives: 46 us -> 64.6 us  [the longest x1 35.3 us: per_device(): rows = lax.all_to_all(sent, 'feat', 0, 0).reshape(tokens, sent.shape[2])]
    dot_general x2 -> x1, matrix products: 16.8 us -> 1.85 us  [per_device(): jnp.dot(rows[:, depth:depth + span], skip_weight[0], preferred_element_ty...]
    all_gather x1 -> x0, blocking collectives: 14.9 us -> none  [per_device(): shards = lax.all_gather(acts_in[0], 'layer', axis=0)]
    ppermute x0 -> x8, starting transfers between devices: none -> 13.4 us  [the longest x3 9.33 us: per_device(): lax.ppermute(pair[s], 'layer', [(i, i + 2 * s) for i in range(layers - 2...]
    ppermute x0 -> x8, waiting for transfers between devices: none -> 12.2 us  [the longest x3 8.89 us: per_device(): lax.ppermute(acts_in[0], 'layer', [(i, i - 2 * s) for i in range(2 * s, l...]
    reduce_scatter x1 -> x2, waiting for transfers between devices: 0.02 us -> 8.66 us  [the longest x1 8.66 us: per_device(): lax.psum_scatter(halfway.astype(F32), 'feat', scatter_dimension=0, axis_i...]
  transfers between devices with their start and end apart: 3 -> 10, of which waited for: 2 -> 7; matrix products, arithmetic and copies ran while one was open for 7% -> 2% of each run, Pallas kernels for 30% -> 10%
where the time goes in v2:
time: 143 us
  blocking collectives  64.6 us (45%)
  waiting for transfers between devices  20.9 us (15%)
  Pallas kernels  19.3 us (13%)
  between operations  13.6 us (10%)
  starting transfers between devices  13.5 us (9%)
  other arithmetic  4.51 us (3%)
  local copies, waits for them, and re-layouts  4.3 us (3%)
  matrix products  1.85 us (1%)
    all_to_all x1, blocking collectives, per_device(): rows = lax.all_to_all(sent, 'feat', 0, 0).reshape(tokens, sent.shape[2])  35.3 us
    all_to_all x1, blocking collectives, per_device(): lax.all_to_all(part.reshape(width, shard, depth // PIECES), 'feat', 0, 0)  29.4 us
    pallas_call x1, Pallas kernels, encode_decode(): pl.pallas_call(kernel, out_shape=[jax.ShapeDtypeStruct((tokens, features)...  14.9 us
    ppermute x3, starting transfers between devices, per_device(): lax.ppermute(pair[s], 'layer', [(i, i + 2 * s) for i in range(layers - 2...  9.33 us
    ppermute x3, waiting for transfers between devices, per_device(): lax.ppermute(acts_in[0], 'layer', [(i, i - 2 * s) for i in range(2 * s, l...  8.89 us
    reduce_scatter x1, waiting for transfers between devices, per_device(): lax.psum_scatter(halfway.astype(F32), 'feat', scatter_dimension=0, axis_i...  8.66 us
    ppermute x3, starting transfers between devices, per_device(): lax.ppermute(acts_in[0], 'layer', [(i, i - 2 * s) for i in range(2 * s, l...  4 us
    pallas_call x1, Pallas kernels, sum_by_place(): pl.pallas_call(kernel, grid=(width // step,), out_shape=[jax.ShapeDtypeSt...  3.6 us
  transfers between devices with their start and end apart: 10, of which 7 were waited for; matrix products, arithmetic and copies ran while one was open for 2% of the time, Pallas kernels for 10%

profile of v2, /device:TPU:0, one launch (start us, length us, event | category | flops | bytes accessed | tf_op | source)
XLA Modules:
  0.0 142.6 jit_solution(16384817844465010172)
XLA Ops:
  6.5 0.0 copy-start
  6.5 0.0 reduce-scatter.3.cloned.1.call-start
  6.5 1.4 collective-permute-start
  8.0 1.3 collective-permute-start.1
  9.3 1.3 collective-permute-start.2
  10.6 3.0 %collective-permute-done = bf16[16,3584]{1,0:T(8,128)(2,1)S(1)} collective-permute-done((bf16[16,3584]{1,0:T(8,128)(2,1)}, bf16[16,3584]{1,0:T(8,128)(2,1)S(1)}, u32[]{:S(2)}, u32[]{:S(2)}) %collective-permute-start) | collective-permute-done | bytes 114720 | tf_op jit(solution)/shard_map/ppermute | solution.py:168
  13.6 3.0 %collective-permute-done.1 = bf16[16,3584]{1,0:T(8,128)(2,1)S(1)} collective-permute-done((bf16[16,3584]{1,0:T(8,128)(2,1)}, bf16[16,3584]{1,0:T(8,128)(2,1)S(1)}, u32[]{:S(2)}, u32[]{:S(2)}) %collective-permute-start.1) | collective-permute-done | bytes 114720 | tf_op jit(solution)/shard_map/ppermute | solution.py:168
  16.6 2.9 %collective-permute-done.2 = bf16[16,3584]{1,0:T(8,128)(2,1)S(1)} collective-permute-done((bf16[16,3584]{1,0:T(8,128)(2,1)}, bf16[16,3584]{1,0:T(8,128)(2,1)S(1)}, u32[]{:S(2)}, u32[]{:S(2)}) %collective-permute-start.2) | collective-permute-done | bytes 114720 | tf_op jit(solution)/shard_map/ppermute | solution.py:168
  19.5 1.0 pad_maximum_fusion.near_ref
  20.4 0.1 collective-permute-start.3
  20.5 1.1 reshape_squeeze.3
  21.7 0.7 fusion.8.place_ref
  22.5 0.0 collective-permute-done.3.far_ref
  22.5 0.9 shard_map.82
  23.3 35.3 %all_to_all.10 = bf16[16,16,3840]{2,1,0:T(8,128)(2,1)S(1)} all-to-all(bf16[16,16,3840]{2,1,0:T(8,128)(2,1)S(1)} %shard_map.82), channel_id=1, replica_groups=mesh['layer'=8,'feat'=16] {'feat'}, dimensions={0} | all-to-all | bytes 3932160 | tf_op jit(solution)/shard_map/all_to_all | solution.py:173
  58.6 0.0 copy-start.4
  58.6 1.3 copy-done.4
  59.9 0.0 copy-done
  59.9 1.9 %convolution_convert_fusion.after_ref = bf16[256,3584]{1,0:T(8,128)(2,1)} fusion(bf16[1,224,3584]{2,1,0:T(8,128)(2,1)S(1)} %copy-done, bf16[256,3840]{1,0:T(8,128)(2,1)S(1)} %bitcast.29), kind=kOutput, calls=%fused_computation | convolution fusion | flops 411959296 | bytes 3571712 | tf_op jit(solution)/shard_map/dot_general | solution.py:174
  61.7 0.0 reduce-scatter.3.cloned.1.call-update
  61.8 0.0 reduce-scatter.5.cloned.1.call-start
  61.8 14.9 %shard_map.83 = (bf16[256,1536]{1,0:T(8,128)(2,1)}, bf16[256,3584]{1,0:T(8,128)(2,1)}) custom-call(bf16[256,3840]{1,0:T(8,128)(2,1)} %bitcast.30, bf16[1,3584,1536]{2,1,0:T(8,128)(2,1)} %enc_ref.1, f32[1,1536]{1,0:T(1,128)} %thr_ref.1, bf16[1,1536,3584]{2,1,0:T(8,128)(2,1)} %dec_ref.1, bf16[256,3584]{1,0:T(8,128)(2,1)} %convolution_convert_fusion.after_ref), custom_call_target="tpu_custom_call" | custom-call | flops 5637144576 | bytes 22020096 | tf_op jit(solution)/shard_map/pallas_call | solution.py:106
  76.7 29.4 %all_to_all.11.parts_ref = bf16[16,16,3584]{2,1,0:T(8,128)(2,1)S(1)} all-to-all(bf16[16,16,3584]{2,1,0:T(8,128)(2,1)} %bitcast.31), channel_id=1, replica_groups=mesh['layer'=8,'feat'=16] {'feat'}, dimensions={0} | all-to-all | bytes 3670016 | tf_op jit(solution)/shard_map/all_to_all | solution.py:185
  106.1 0.0 reduce-scatter.3.cloned.1.call-done.after_ref
  106.1 0.0 copy-start.1
  106.1 1.0 copy-done.1
  107.1 3.6 %shard_map.84 = (bf16[4,16,3584]{2,1,0:T(8,128)(2,1)S(1)}, bf16[4,16,3584]{2,1,0:T(8,128)(2,1)}) custom-call(s32[16]{0:T(128)S(1)} %fusion.8.place_ref, bf16[16,16,3584]{2,1,0:T(8,128)(2,1)S(1)} %all_to_all.11.parts_ref, bf16[64,3584]{1,0:T(8,128)(2,1)S(1)} %copy-done.1), custom_call_target="tpu_custom_call" | custom-call | flops 917504 | bytes 2752512 | tf_op jit(solution)/shard_map/pallas_call | solution.py:65
  110.7 0.0 copy-start.2
  110.7 0.8 copy-done.2
  111.5 0.0 copy-start.3
  111.5 0.0 collective-permute-start.4
  111.5 1.0 convert_element_type.49
  112.5 0.0 copy-start.6
  112.5 0.0 copy-start.5
  112.5 0.0 reduce-scatter.5.cloned.1.call-update
  112.5 1.0 collective-permute-done.4
  113.5 0.0 copy-done.3
  113.5 0.1 add_convert_fusion
  113.6 3.4 %collective-permute-start.5 = (bf16[16,3584]{1,0:T(8,128)(2,1)S(1)}, bf16[16,3584]{1,0:T(8,128)(2,1)S(1)}, u32[]{:S(2)}, u32[]{:S(2)}) collective-permute-start(bf16[16,3584]{1,0:T(8,128)(2,1)S(1)} %get-tuple-element.11), channel_id=1, source_target_pairs={{0,32},{16,48},{32,64},{48,80},{64,96},{80,112},{1,33},{17,49},{33... | collective-permute-start | bytes 344072 | tf_op jit(solution)/shard_map/ppermute | solution.py:192
  117.0 4.7 %collective-permute-start.6 = (bf16[16,3584]{1,0:T(8,128)(2,1)S(1)}, bf16[16,3584]{1,0:T(8,128)(2,1)S(1)}, u32[]{:S(2)}, u32[]{:S(2)}) collective-permute-start(bf16[16,3584]{1,0:T(8,128)(2,1)S(1)} %get-tuple-element.13), channel_id=1, source_target_pairs={{0,64},{16,80},{32,96},{48,112},{1,65},{17,81},{33,97},{49,113},{2... | collective-permute-start | bytes 344072 | tf_op jit(solution)/shard_map/ppermute | solution.py:192
  121.7 1.3 collective-permute-start.7
  123.0 0.0 copy-done.6
  123.1 0.0 collective-permute-done.5
  123.1 1.0 collective-permute-done.6
  124.1 1.3 collective-permute-done.7
  125.4 8.7 %reduce-scatter.5.cloned.1.call-done = f32[16,3584]{1,0:T(8,128)} async-done(((f32[64,3584]{1,0:T(8,128)}), f32[16,3584]{1,0:T(8,128)}) %reduce-scatter.5.cloned.1.call-update) | async-done | bytes 229392 | tf_op jit(solution)/shard_map/reduce_scatter | solution.py:180
  134.1 0.0 copy-done.5
  134.1 1.7 %fusion.7 = bf16[1,16,3584]{2,1,0:T(8,128)(2,1)} fusion(f32[16,3584]{1,0:T(8,128)} %reduce-scatter.5.cloned.1.call-done, bf16[16,3584]{1,0:T(8,128)(2,1)S(1)} %collective-permute-done.7, bf16[16,3584]{1,0:T(8,128)(2,1)S(1)} %collective-permute-done.6, bf16[16,3584]{1,0:T(8,128)(2,1)S(1)} %collective-permute-done.5, ...), kind=kLoop, calls=%fused_computation.13 | loop fusion | flops 688128 | bytes 931840 | tf_op jit(solution)/shard_map/broadcast_in_dim | solution.py:197
  (3 shorter events, 0.1 us)
Async XLA Ops:
  6.5 53.3 %copy-start = (bf16[1,224,3584]{2,1,0:T(8,128)(2,1)S(1)}, bf16[1,224,3584]{2,1,0:T(8,128)(2,1)}, u32[]{:S(2)}) copy-start(bf16[1,224,3584]{2,1,0:T(8,128)(2,1)} %param.13) | copy-start | bytes 4816900
  6.5 99.5 %reduce-scatter.3.cloned.1.call-start = ((), (), s32[]{:S(2)}) async-start(), calls=%async_computation.4 | async-start | bytes 2293760 | tf_op jit(solution)/shard_map/reduce_scatter | solution.py:177
  6.5 7.0 %collective-permute-start = (bf16[16,3584]{1,0:T(8,128)(2,1)}, bf16[16,3584]{1,0:T(8,128)(2,1)S(1)}, u32[]{:S(2)}, u32[]{:S(2)}) collective-permute-start(bf16[16,3584]{1,0:T(8,128)(2,1)} %bitcast.32), channel_id=1, source_target_pairs={{32,0},{48,16},{64,32},{80,48},{96,64},{112,80},{33,1},{49,17},{65... | collective-permute-start | bytes 344072 | tf_op jit(solution)/shard_map/ppermute | solution.py:168
  8.0 8.6 %collective-permute-start.1 = (bf16[16,3584]{1,0:T(8,128)(2,1)}, bf16[16,3584]{1,0:T(8,128)(2,1)S(1)}, u32[]{:S(2)}, u32[]{:S(2)}) collective-permute-start(bf16[16,3584]{1,0:T(8,128)(2,1)} %bitcast.33), channel_id=1, source_target_pairs={{64,0},{80,16},{96,32},{112,48},{65,1},{81,17},{97,33},{113,49},{6... | collective-permute-start | bytes 344072 | tf_op jit(solution)/shard_map/ppermute | solution.py:168
  9.3 10.2 %collective-permute-start.2 = (bf16[16,3584]{1,0:T(8,128)(2,1)}, bf16[16,3584]{1,0:T(8,128)(2,1)S(1)}, u32[]{:S(2)}, u32[]{:S(2)}) collective-permute-start(bf16[16,3584]{1,0:T(8,128)(2,1)} %bitcast.34), channel_id=1, source_target_pairs={{96,0},{112,16},{97,1},{113,17},{98,2},{114,18},{99,3},{115,19},{1... | collective-permute-start | bytes 344072 | tf_op jit(solution)/shard_map/ppermute | solution.py:168
  20.4 2.0 %collective-permute-start.3 = (bf16[4,16,3584]{2,1,0:T(8,128)(2,1)S(1)}, bf16[4,16,3584]{2,1,0:T(8,128)(2,1)S(1)}, u32[]{:S(2)}, u32[]{:S(2)}) collective-permute-start(bf16[4,16,3584]{2,1,0:T(8,128)(2,1)S(1)} %pad_maximum_fusion.near_ref), channel_id=1, source_target_pairs={{0,16},{16,0},{32,48},{48,32},{64,80},{80,64},{96,112},{112,96},{1... | collective-permute-start | bytes 1376264 | tf_op jit(solution)/shard_map/ppermute | solution.py:171
  58.6 1.3 copy-start.4
  61.8 72.3 %reduce-scatter.5.cloned.1.call-start = ((), (), s32[]{:S(2)}) async-start(), calls=%async_computation.5 | async-start | bytes 1146880 | tf_op jit(solution)/shard_map/reduce_scatter | solution.py:180
  106.1 1.0 copy-start.1
  110.7 0.8 copy-start.2
  111.5 2.0 %copy-start.3 = (bf16[4,16,3584]{2,1,0:T(8,128)(2,1)S(1)}, bf16[4,16,3584]{2,1,0:T(8,128)(2,1)}, u32[]{:S(2)}) copy-start(bf16[4,16,3584]{2,1,0:T(8,128)(2,1)} %copy-done.2) | copy-start | bytes 1376260
  111.5 2.0 %collective-permute-start.4 = (bf16[4,16,3584]{2,1,0:T(8,128)(2,1)}, bf16[4,16,3584]{2,1,0:T(8,128)(2,1)S(1)}, u32[]{:S(2)}, u32[]{:S(2)}) collective-permute-start(bf16[4,16,3584]{2,1,0:T(8,128)(2,1)} %get-tuple-element.10), channel_id=1, source_target_pairs={{0,16},{16,0},{32,48},{48,32},{64,80},{80,64},{96,112},{112,96},{1... | collective-permute-start | bytes 1376264 | tf_op jit(solution)/shard_map/ppermute | solution.py:189
  112.5 10.5 %copy-start.6 = (f32[1,3584]{1,0:T(1,128)S(1)}, f32[1,3584]{1,0:T(1,128)}, u32[]{:S(2)}) copy-start(f32[1,3584]{1,0:T(1,128)} %param.14) | copy-start | bytes 43012
  112.5 21.6 %copy-start.5 = (bf16[1,16,3584]{2,1,0:T(8,128)(2,1)S(1)}, bf16[1,16,3584]{2,1,0:T(8,128)(2,1)}, u32[]{:S(2)}) copy-start(bf16[1,16,3584]{2,1,0:T(8,128)(2,1)} %param.9) | copy-start | bytes 344068
  113.6 9.4 %collective-permute-start.5 = (bf16[16,3584]{1,0:T(8,128)(2,1)S(1)}, bf16[16,3584]{1,0:T(8,128)(2,1)S(1)}, u32[]{:S(2)}, u32[]{:S(2)}) collective-permute-start(bf16[16,3584]{1,0:T(8,128)(2,1)S(1)} %get-tuple-element.11), channel_id=1, source_target_pairs={{0,32},{16,48},{32,64},{48,80},{64,96},{80,112},{1,33},{17,49},{33... | collective-permute-start | bytes 344072 | tf_op jit(solution)/shard_map/ppermute | solution.py:192
  117.0 7.1 %collective-permute-start.6 = (bf16[16,3584]{1,0:T(8,128)(2,1)S(1)}, bf16[16,3584]{1,0:T(8,128)(2,1)S(1)}, u32[]{:S(2)}, u32[]{:S(2)}) collective-permute-start(bf16[16,3584]{1,0:T(8,128)(2,1)S(1)} %get-tuple-element.13), channel_id=1, source_target_pairs={{0,64},{16,80},{32,96},{48,112},{1,65},{17,81},{33,97},{49,113},{2... | collective-permute-start | bytes 344072 | tf_op jit(solution)/shard_map/ppermute | solution.py:192
  121.7 3.7 %collective-permute-start.7 = (bf16[16,3584]{1,0:T(8,128)(2,1)S(1)}, bf16[16,3584]{1,0:T(8,128)(2,1)S(1)}, u32[]{:S(2)}, u32[]{:S(2)}) collective-permute-start(bf16[16,3584]{1,0:T(8,128)(2,1)S(1)} %get-tuple-element.12), channel_id=1, source_target_pairs={{0,96},{16,112},{1,97},{17,113},{2,98},{18,114},{3,99},{19,115},{4... | collective-permute-start | bytes 344072 | tf_op jit(solution)/shard_map/ppermute | solution.py:192
Sparse Core Ops, SparseCore 0:
  61.9 24.1 reduce-scatter.2
  112.6 21.4 reduce-scatter.4

commit v3 on v2

--- a/solution.py
+++ b/solution.py
@@ -148,6 +148,24 @@
     )(act, dec, after)
 
 
+def skip_product(rows, weight, start, begin, width, after):
+    tokens, span = rows.shape[0], weight.shape[1]
+
+    def kernel(rows_ref, weight_ref, after_ref, out_ref):
+        out_ref[...] = jnp.dot(
+            rows_ref[:, start : start + span], weight_ref[0, :, begin : begin + width], preferred_element_type=F32
+        ).astype(BF)
+
+    return pl.pallas_call(
+        kernel,
+        out_shape=jax.ShapeDtypeStruct((tokens, width), BF),
+        in_specs=[whole(pltpu.VMEM), whole(pltpu.VMEM), whole(pl.ANY)],
+        out_specs=whole(pltpu.VMEM),
+        compiler_params=pltpu.CompilerParams(vmem_limit_bytes=VMEM_LIMIT),
+        cost_estimate=pl.CostEstimate(flops=2 * tokens * span * width, bytes_accessed=(tokens + span) * width * 2, transcendentals=0),
+    )(rows, weight, after)
+
+
 PIECES = 1
 
 
@@ -171,28 +189,27 @@
     far = lax.ppermute(near, "layer", swap)
     sent = pick_rows(near, far, place, cut)
     rows = lax.all_to_all(sent, "feat", 0, 0).reshape(tokens, sent.shape[2])
-    skipped = jnp.dot(rows[:, depth : depth + span], skip_weight[0], preferred_element_type=F32).astype(BF)
-    by_across = [[y * down + z for y in range(across)] for z in range(down)]
-    by_down = [[y * down + z for z in range(down)] for y in range(across)]
-    halfway = lax.psum_scatter(skipped, "feat", scatter_dimension=0, axis_index_groups=by_across, tiled=True)
-
-    act, part = encode_decode(rows, enc_weight, thresholds, dec_weight, depth // PIECES, skipped)
-    skip_sum = lax.psum_scatter(halfway.astype(F32), "feat", scatter_dimension=0, axis_index_groups=by_down, tiled=True)
-    parts = [part]
-    if PIECES == 2:
-        parts.append(decode_rest(act, dec_weight, depth // PIECES, halfway))
-
-    backs = [lax.all_to_all(part.reshape(width, shard, depth // PIECES), "feat", 0, 0) for part in parts]
-    outs = []
-    for back in backs:
-        kept, given = sum_by_place(back, place, chips, outs[-1] if outs else halfway)
-        taken = lax.ppermute(given, "layer", swap)
-        pair = (kept.astype(F32) + taken.astype(F32)).astype(BF)
-        arrived = [
-            lax.ppermute(pair[s], "layer", [(i, i + 2 * s) for i in range(layers - 2 * s)]) for s in range(1, chips)
-        ]
-        outs.append(sum((a.astype(F32) for a in arrived), pair[0].astype(F32)))
-    recon = jnp.concatenate(outs, axis=1) + skip_sum
+    half = depth // 2
+    skip_a = skip_product(rows, skip_weight, depth, 0, half, place)
+    skip_a_back = lax.all_to_all(skip_a.reshape(width, shard, half), "feat", 0, 0)
+
+    _, part = encode_decode(rows, enc_weight, thresholds, dec_weight, depth, skip_a)
+    part, skip_a_back = lax.optimization_barrier((part, skip_a_back))
+
+    back = lax.all_to_all(part.reshape(width, shard, depth), "feat", 0, 0)
+    skip_b = skip_product(rows, skip_weight, depth, half, half, back)
+    skip_b_back = lax.all_to_all(skip_b.reshape(width, shard, half), "feat", 0, 0)
+    kept, given = sum_by_place(back, place, chips, skip_b)
+    taken = lax.ppermute(given, "layer", swap)
+    pair = (kept.astype(F32) + taken.astype(F32)).astype(BF)
+    arrived = [
+        lax.ppermute(pair[s], "layer", [(i, i + 2 * s) for i in range(layers - 2 * s)]) for s in range(1, chips)
+    ]
+    recon = sum((a.astype(F32) for a in arrived), pair[0].astype(F32))
+    skip_sum = jnp.concatenate(
+        [jnp.sum(skip_a_back.astype(F32), axis=0), jnp.sum(skip_b_back.astype(F32), axis=0)], axis=1
+    )
+    recon = recon + skip_sum
     total = recon + dec_bias[0][None, :] - targets[0].astype(F32)
     return total.astype(BF)[None]
 

time: 143 us -> 130 us (0.909)
  between operations: 13.6 us -> 0.27 us
  starting transfers between devices: 13.5 us -> 17.8 us
  local copies, waits for them, and re-layouts: 4.3 us -> 1.2 us
  matrix products: 1.85 us -> 0 us
  blocking collectives: 64.6 us -> 66.4 us
  other arithmetic: 4.51 us -> 2.84 us
    all_to_all x0 -> x2, waiting for transfers between devices: none -> 11.4 us  [the longest x1 10.6 us: per_device(): lax.all_to_all(skip_b.reshape(width, shard, half), 'feat', 0, 0)]
    reduce_scatter x2 -> x0, waiting for transfers between devices: 8.66 us -> none  [the longest x1 8.66 us: per_device(): lax.psum_scatter(halfway.astype(F32), 'feat', scatter_dimension=0, axis_i...]
    all_to_all x0 -> x2, starting transfers between devices: none -> 7.36 us  [the longest x1 3.72 us: per_device(): lax.all_to_all(skip_a.reshape(width, shard, half), 'feat', 0, 0)]
    unnamed x14 -> x12, local copies, waits for them, and re-layouts: 3.13 us -> 0.03 us
    ppermute x3, starting transfers between devices: 9.33 us -> 6.36 us  [per_device(): lax.ppermute(pair[s], 'layer', [(i, i + 2 * s) for i in range(layers - 2...]
    pallas_call x0 -> x2, Pallas kernels: none -> 2.95 us  [skip_product(): pl.pallas_call(kernel, out_shape=jax.ShapeDtypeStruct((tokens, width), BF...]
    ppermute x3, waiting for transfers between devices: 2.34 us -> 0.01 us  [per_device(): lax.ppermute(pair[s], 'layer', [(i, i + 2 * s) for i in range(layers - 2...]
    pallas_call x1, Pallas kernels: 3.6 us -> 1.67 us  [sum_by_place(): pl.pallas_call(kernel, grid=(width // step,), out_shape=[jax.ShapeDtypeSt...]
  transfers between devices with their start and end apart: 10 -> 10, of which waited for: 7 -> 5; matrix products, arithmetic and copies ran while one was open for 2% -> 2% of each run, Pallas kernels for 10% -> 11%
where the time goes in v3:
time: 130 us; the launch traced here: 129 us
  blocking collectives  66.4 us (51%)
  waiting for transfers between devices  20.3 us (16%)
  Pallas kernels  20 us (15%)
  starting transfers between devices  17.8 us (14%)
  other arithmetic  2.84 us (2%)
    all_to_all x1, blocking collectives, per_device(): rows = lax.all_to_all(sent, 'feat', 0, 0).reshape(tokens, sent.shape[2])  35.4 us
    all_to_all x1, blocking collectives, per_device(): back = lax.all_to_all(part.reshape(width, shard, depth), 'feat', 0, 0)  31 us
    pallas_call x1, Pallas kernels, encode_decode(): pl.pallas_call(kernel, out_shape=[jax.ShapeDtypeStruct((tokens, features)...  14.5 us
    all_to_all x1, waiting for transfers between devices, per_device(): lax.all_to_all(skip_b.reshape(width, shard, half), 'feat', 0, 0)  10.6 us
    ppermute x3, waiting for transfers between devices, per_device(): lax.ppermute(acts_in[0], 'layer', [(i, i - 2 * s) for i in range(2 * s, l...  8.89 us
    ppermute x3, starting transfers between devices, per_device(): lax.ppermute(pair[s], 'layer', [(i, i + 2 * s) for i in range(layers - 2...  6.36 us
    ppermute x3, starting transfers between devices, per_device(): lax.ppermute(acts_in[0], 'layer', [(i, i - 2 * s) for i in range(2 * s, l...  3.86 us
    all_to_all x1, starting transfers between devices, per_device(): lax.all_to_all(skip_a.reshape(width, shard, half), 'feat', 0, 0)  3.72 us
  transfers between devices with their start and end apart: 10, of which 5 were waited for; matrix products, arithmetic and copies ran while one was open for 2% of the time, Pallas kernels for 11%

profile of v3, /device:TPU:0, one launch (start us, length us, event | category | flops | bytes accessed | tf_op | source)
XLA Modules:
  0.0 128.8 jit_solution(7754599019961755359)
XLA Ops:
  0.0 1.3 collective-permute-start
  1.3 1.3 %collective-permute-start.1 = (bf16[16,3584]{1,0:T(8,128)(2,1)}, bf16[16,3584]{1,0:T(8,128)(2,1)S(1)}, u32[]{:S(2)}, u32[]{:S(2)}) collective-permute-start(bf16[16,3584]{1,0:T(8,128)(2,1)} %bitcast.37), channel_id=1, source_target_pairs={{64,0},{80,16},{96,32},{112,48},{65,1},{81,17},{97,33},{113,49},{6... | collective-permute-start | bytes 344072 | tf_op jit(solution)/shard_map/ppermute | solution.py:186
  2.6 1.3 %collective-permute-start.2 = (bf16[16,3584]{1,0:T(8,128)(2,1)}, bf16[16,3584]{1,0:T(8,128)(2,1)S(1)}, u32[]{:S(2)}, u32[]{:S(2)}) collective-permute-start(bf16[16,3584]{1,0:T(8,128)(2,1)} %bitcast.38), channel_id=1, source_target_pairs={{96,0},{112,16},{97,1},{113,17},{98,2},{114,18},{99,3},{115,19},{1... | collective-permute-start | bytes 344072 | tf_op jit(solution)/shard_map/ppermute | solution.py:186
  3.9 3.0 %collective-permute-done = bf16[16,3584]{1,0:T(8,128)(2,1)S(1)} collective-permute-done((bf16[16,3584]{1,0:T(8,128)(2,1)}, bf16[16,3584]{1,0:T(8,128)(2,1)S(1)}, u32[]{:S(2)}, u32[]{:S(2)}) %collective-permute-start) | collective-permute-done | bytes 114720 | tf_op jit(solution)/shard_map/ppermute | solution.py:186
  6.9 3.0 %collective-permute-done.1 = bf16[16,3584]{1,0:T(8,128)(2,1)S(1)} collective-permute-done((bf16[16,3584]{1,0:T(8,128)(2,1)}, bf16[16,3584]{1,0:T(8,128)(2,1)S(1)}, u32[]{:S(2)}, u32[]{:S(2)}) %collective-permute-start.1) | collective-permute-done | bytes 114720 | tf_op jit(solution)/shard_map/ppermute | solution.py:186
  9.9 2.9 %collective-permute-done.2 = bf16[16,3584]{1,0:T(8,128)(2,1)S(1)} collective-permute-done((bf16[16,3584]{1,0:T(8,128)(2,1)}, bf16[16,3584]{1,0:T(8,128)(2,1)S(1)}, u32[]{:S(2)}, u32[]{:S(2)}) %collective-permute-start.2) | collective-permute-done | bytes 114720 | tf_op jit(solution)/shard_map/ppermute | solution.py:186
  12.8 1.0 pad_maximum_fusion.near_ref
  13.7 0.1 collective-permute-start.3
  13.8 1.1 reshape_squeeze.3
  15.0 0.7 fusion.6.place_ref.after_ref
  15.8 0.0 collective-permute-done.3.far_ref
  15.8 0.9 shard_map.82
  16.6 0.0 copy-start.2
  16.7 35.4 %all_to_all.20 = bf16[16,16,3840]{2,1,0:T(8,128)(2,1)S(1)} all-to-all(bf16[16,16,3840]{2,1,0:T(8,128)(2,1)S(1)} %shard_map.82), channel_id=1, replica_groups=mesh['layer'=8,'feat'=16] {'feat'}, dimensions={0} | all-to-all | bytes 3932160 | tf_op jit(solution)/shard_map/all_to_all | solution.py:191
  52.0 0.0 copy-start
  52.0 0.0 copy-done.2
  52.0 1.6 %shard_map.83.after_ref = bf16[256,1792]{1,0:T(8,128)(2,1)} custom-call(bf16[256,3840]{1,0:T(8,128)(2,1)S(1)} %bitcast.31, bf16[1,224,3584]{2,1,0:T(8,128)(2,1)S(1)} %copy-done.2, s32[16]{0:T(128)S(1)} %fusion.6.place_ref.after_ref), custom_call_target="tpu_custom_call" | custom-call | flops 205520896 | bytes 1720320 | tf_op jit(solution)/shard_map/pallas_call | solution.py:159
  53.7 0.0 copy-done
  53.7 3.7 %all-to-all-start.1 = ((bf16[16,16,1792]{2,1,0:T(8,128)(2,1)}), bf16[16,16,1792]{2,1,0:T(8,128)(2,1)S(1)}, u32[]{:S(2)}, u32[]{:S(2)}) async-start(bf16[16,16,1792]{2,1,0:T(8,128)(2,1)} %bitcast.6), calls=%async_computation.1 | async-start | bytes 1835008 | tf_op jit(solution)/shard_map/all_to_all | solution.py:194
  57.4 14.5 %shard_map.84 = (bf16[256,1536]{1,0:T(8,128)(2,1)}, bf16[256,3584]{1,0:T(8,128)(2,1)}) custom-call(bf16[256,3840]{1,0:T(8,128)(2,1)} %bitcast.32, bf16[1,3584,1536]{2,1,0:T(8,128)(2,1)} %enc_ref.1, f32[1,1536]{1,0:T(1,128)} %thr_ref.1, bf16[1,1536,3584]{2,1,0:T(8,128)(2,1)} %dec_ref.1, bf16[256,1792]{1,0:T(8,128)(2,1)} %shard_map.83.after_ref), custom_call_target="tpu_custom_call" | custom-call | flops 5637144576 | bytes 22020096 | tf_op jit(solution)/shard_map/pallas_call | solution.py:106
  71.9 0.8 all-to-all-done.1
  72.7 0.0 copy-start.1
  72.7 0.0 copy-start.3
  72.7 31.0 %all_to_all.21.after_ref.parts_ref = bf16[16,16,3584]{2,1,0:T(8,128)(2,1)S(1)} all-to-all(bf16[16,16,3584]{2,1,0:T(8,128)(2,1)} %bitcast.35), channel_id=1, replica_groups=mesh['layer'=8,'feat'=16] {'feat'}, dimensions={0} | all-to-all | bytes 3670016 | tf_op jit(solution)/shard_map/all_to_all | solution.py:199
  103.8 0.0 copy-done.1
  103.8 0.0 copy-done.3
  103.8 1.3 %shard_map.85.after_ref = bf16[256,1792]{1,0:T(8,128)(2,1)} custom-call(bf16[256,3840]{1,0:T(8,128)(2,1)S(1)} %bitcast.33, bf16[1,224,3584]{2,1,0:T(8,128)(2,1)S(1)} %copy-done.3, bf16[16,16,3584]{2,1,0:T(8,128)(2,1)S(1)} %all_to_all.21.after_ref.parts_ref), custom_call_target="tpu_custom_call" | custom-call | flops 205520896 | bytes 1720320 | tf_op jit(solution)/shard_map/pallas_call | solution.py:159
  105.1 0.0 copy-start.5
  105.1 1.7 %shard_map.86 = (bf16[4,16,3584]{2,1,0:T(8,128)(2,1)S(1)}, bf16[4,16,3584]{2,1,0:T(8,128)(2,1)S(1)}) custom-call(s32[16]{0:T(128)S(1)} %fusion.6.place_ref.after_ref, bf16[16,16,3584]{2,1,0:T(8,128)(2,1)S(1)} %all_to_all.21.after_ref.parts_ref, bf16[256,1792]{1,0:T(8,128)(2,1)} %shard_map.85.after_ref), custom_call_target="tpu_custom_call" | custom-call | flops 917504 | bytes 2752512 | tf_op jit(solution)/shard_map/pallas_call | solution.py:65
  106.8 0.1 collective-permute-start.4
  106.9 0.0 copy-done.5
  106.9 0.1 convert_reduce_fusion.1
  107.0 3.6 %all-to-all-start.3 = ((bf16[16,16,1792]{2,1,0:T(8,128)(2,1)}), bf16[16,16,1792]{2,1,0:T(8,128)(2,1)S(1)}, u32[]{:S(2)}, u32[]{:S(2)}) async-start(bf16[16,16,1792]{2,1,0:T(8,128)(2,1)} %bitcast.12), calls=%async_computation.3 | async-start | bytes 1835008 | tf_op jit(solution)/shard_map/all_to_all | solution.py:201
  110.7 0.0 copy-start.4
  110.7 0.0 collective-permute-done.4
  110.7 0.1 add_convert_fusion
  110.9 1.4 %collective-permute-start.5 = (bf16[16,3584]{1,0:T(8,128)(2,1)S(1)}, bf16[16,3584]{1,0:T(8,128)(2,1)S(1)}, u32[]{:S(2)}, u32[]{:S(2)}) collective-permute-start(bf16[16,3584]{1,0:T(8,128)(2,1)S(1)} %get-tuple-element.15), channel_id=1, source_target_pairs={{0,32},{16,48},{32,64},{48,80},{64,96},{80,112},{1,33},{17,49},{33... | collective-permute-start | bytes 344072 | tf_op jit(solution)/shard_map/ppermute | solution.py:206
  112.3 3.6 %collective-permute-start.6 = (bf16[16,3584]{1,0:T(8,128)(2,1)S(1)}, bf16[16,3584]{1,0:T(8,128)(2,1)S(1)}, u32[]{:S(2)}, u32[]{:S(2)}) collective-permute-start(bf16[16,3584]{1,0:T(8,128)(2,1)S(1)} %get-tuple-element.17), channel_id=1, source_target_pairs={{0,64},{16,80},{32,96},{48,112},{1,65},{17,81},{33,97},{49,113},{2... | collective-permute-start | bytes 344072 | tf_op jit(solution)/shard_map/ppermute | solution.py:206
  116.0 1.3 %collective-permute-start.7 = (bf16[16,3584]{1,0:T(8,128)(2,1)S(1)}, bf16[16,3584]{1,0:T(8,128)(2,1)S(1)}, u32[]{:S(2)}, u32[]{:S(2)}) collective-permute-start(bf16[16,3584]{1,0:T(8,128)(2,1)S(1)} %get-tuple-element.16), channel_id=1, source_target_pairs={{0,96},{16,112},{1,97},{17,113},{2,98},{18,114},{3,99},{19,115},{4... | collective-permute-start | bytes 344072 | tf_op jit(solution)/shard_map/ppermute | solution.py:206
  117.3 10.6 %all-to-all-done.3 = bf16[16,16,1792]{2,1,0:T(8,128)(2,1)S(1)} async-done(((bf16[16,16,1792]{2,1,0:T(8,128)(2,1)}), bf16[16,16,1792]{2,1,0:T(8,128)(2,1)S(1)}, u32[]{:S(2)}, u32[]{:S(2)}) %all-to-all-start.3) | async-done | bytes 917536 | tf_op jit(solution)/shard_map/all_to_all | solution.py:201
  127.9 0.1 convert_reduce_fusion
  128.0 0.0 collective-permute-done.5
  128.0 0.0 collective-permute-done.6
  128.0 0.0 collective-permute-done.7
  128.0 0.0 copy-done.4
  128.1 0.7 fusion.5
  (3 shorter events, 0.1 us)
Async XLA Ops:
  0.0 6.9 %collective-permute-start = (bf16[16,3584]{1,0:T(8,128)(2,1)}, bf16[16,3584]{1,0:T(8,128)(2,1)S(1)}, u32[]{:S(2)}, u32[]{:S(2)}) collective-permute-start(bf16[16,3584]{1,0:T(8,128)(2,1)} %bitcast.36), channel_id=1, source_target_pairs={{32,0},{48,16},{64,32},{80,48},{96,64},{112,80},{33,1},{49,17},{65... | collective-permute-start | bytes 344072 | tf_op jit(solution)/shard_map/ppermute | solution.py:186
  1.3 8.6 %collective-permute-start.1 = (bf16[16,3584]{1,0:T(8,128)(2,1)}, bf16[16,3584]{1,0:T(8,128)(2,1)S(1)}, u32[]{:S(2)}, u32[]{:S(2)}) collective-permute-start(bf16[16,3584]{1,0:T(8,128)(2,1)} %bitcast.37), channel_id=1, source_target_pairs={{64,0},{80,16},{96,32},{112,48},{65,1},{81,17},{97,33},{113,49},{6... | collective-permute-start | bytes 344072 | tf_op jit(solution)/shard_map/ppermute | solution.py:186
  2.6 10.2 %collective-permute-start.2 = (bf16[16,3584]{1,0:T(8,128)(2,1)}, bf16[16,3584]{1,0:T(8,128)(2,1)S(1)}, u32[]{:S(2)}, u32[]{:S(2)}) collective-permute-start(bf16[16,3584]{1,0:T(8,128)(2,1)} %bitcast.38), channel_id=1, source_target_pairs={{96,0},{112,16},{97,1},{113,17},{98,2},{114,18},{99,3},{115,19},{1... | collective-permute-start | bytes 344072 | tf_op jit(solution)/shard_map/ppermute | solution.py:186
  13.7 2.0 %collective-permute-start.3 = (bf16[4,16,3584]{2,1,0:T(8,128)(2,1)S(1)}, bf16[4,16,3584]{2,1,0:T(8,128)(2,1)S(1)}, u32[]{:S(2)}, u32[]{:S(2)}) collective-permute-start(bf16[4,16,3584]{2,1,0:T(8,128)(2,1)S(1)} %pad_maximum_fusion.near_ref), channel_id=1, source_target_pairs={{0,16},{16,0},{32,48},{48,32},{64,80},{80,64},{96,112},{112,96},{1... | collective-permute-start | bytes 1376264 | tf_op jit(solution)/shard_map/ppermute | solution.py:189
  16.6 35.4 %copy-start.2 = (bf16[1,224,3584]{2,1,0:T(8,128)(2,1)S(1)}, bf16[1,224,3584]{2,1,0:T(8,128)(2,1)}, u32[]{:S(2)}) copy-start(bf16[1,224,3584]{2,1,0:T(8,128)(2,1)} %weight_ref.3) | copy-start | bytes 4816900
  52.0 1.6 %copy-start = (bf16[16,16,3840]{2,1,0:T(8,128)(2,1)}, bf16[16,16,3840]{2,1,0:T(8,128)(2,1)S(1)}, u32[]{:S(2)}) copy-start(bf16[16,16,3840]{2,1,0:T(8,128)(2,1)S(1)} %all_to_all.20) | copy-start | bytes 5898244
  53.7 19.0 %all-to-all-start.1 = ((bf16[16,16,1792]{2,1,0:T(8,128)(2,1)}), bf16[16,16,1792]{2,1,0:T(8,128)(2,1)S(1)}, u32[]{:S(2)}, u32[]{:S(2)}) async-start(bf16[16,16,1792]{2,1,0:T(8,128)(2,1)} %bitcast.6), calls=%async_computation.1 | async-start | bytes 1835008 | tf_op jit(solution)/shard_map/all_to_all | solution.py:194
  72.7 31.1 %copy-start.1 = (bf16[16,16,3840]{2,1,0:T(8,128)(2,1)S(1)}, bf16[16,16,3840]{2,1,0:T(8,128)(2,1)}, u32[]{:S(2)}) copy-start(bf16[16,16,3840]{2,1,0:T(8,128)(2,1)} %copy-done) | copy-start | bytes 5898244
  72.7 31.1 %copy-start.3 = (bf16[1,224,3584]{2,1,0:T(8,128)(2,1)S(1)}, bf16[1,224,3584]{2,1,0:T(8,128)(2,1)}, u32[]{:S(2)}) copy-start(bf16[1,224,3584]{2,1,0:T(8,128)(2,1)} %weight_ref.3) | copy-start | bytes 4816900
  105.1 1.8 %copy-start.5 = (f32[1,3584]{1,0:T(1,128)S(1)}, f32[1,3584]{1,0:T(1,128)}, u32[]{:S(2)}) copy-start(f32[1,3584]{1,0:T(1,128)} %param.14) | copy-start | bytes 43012
  106.8 4.0 %collective-permute-start.4 = (bf16[4,16,3584]{2,1,0:T(8,128)(2,1)S(1)}, bf16[4,16,3584]{2,1,0:T(8,128)(2,1)S(1)}, u32[]{:S(2)}, u32[]{:S(2)}) collective-permute-start(bf16[4,16,3584]{2,1,0:T(8,128)(2,1)S(1)} %get-tuple-element.13), channel_id=1, source_target_pairs={{0,16},{16,0},{32,48},{48,32},{64,80},{80,64},{96,112},{112,96},{1... | collective-permute-start | bytes 1376264 | tf_op jit(solution)/shard_map/ppermute | solution.py:203
  107.0 20.8 %all-to-all-start.3 = ((bf16[16,16,1792]{2,1,0:T(8,128)(2,1)}), bf16[16,16,1792]{2,1,0:T(8,128)(2,1)S(1)}, u32[]{:S(2)}, u32[]{:S(2)}) async-start(bf16[16,16,1792]{2,1,0:T(8,128)(2,1)} %bitcast.12), calls=%async_computation.3 | async-start | bytes 1835008 | tf_op jit(solution)/shard_map/all_to_all | solution.py:201
  110.7 17.3 %copy-start.4 = (bf16[1,16,3584]{2,1,0:T(8,128)(2,1)S(1)}, bf16[1,16,3584]{2,1,0:T(8,128)(2,1)}, u32[]{:S(2)}) copy-start(bf16[1,16,3584]{2,1,0:T(8,128)(2,1)} %param.9) | copy-start | bytes 344068
  110.9 17.1 %collective-permute-start.5 = (bf16[16,3584]{1,0:T(8,128)(2,1)S(1)}, bf16[16,3584]{1,0:T(8,128)(2,1)S(1)}, u32[]{:S(2)}, u32[]{:S(2)}) collective-permute-start(bf16[16,3584]{1,0:T(8,128)(2,1)S(1)} %get-tuple-element.15), channel_id=1, source_target_pairs={{0,32},{16,48},{32,64},{48,80},{64,96},{80,112},{1,33},{17,49},{33... | collective-permute-start | bytes 344072 | tf_op jit(solution)/shard_map/ppermute | solution.py:206
  112.3 15.7 %collective-permute-start.6 = (bf16[16,3584]{1,0:T(8,128)(2,1)S(1)}, bf16[16,3584]{1,0:T(8,128)(2,1)S(1)}, u32[]{:S(2)}, u32[]{:S(2)}) collective-permute-start(bf16[16,3584]{1,0:T(8,128)(2,1)S(1)} %get-tuple-element.17), channel_id=1, source_target_pairs={{0,64},{16,80},{32,96},{48,112},{1,65},{17,81},{33,97},{49,113},{2... | collective-permute-start | bytes 344072 | tf_op jit(solution)/shard_map/ppermute | solution.py:206
  116.0 12.1 %collective-permute-start.7 = (bf16[16,3584]{1,0:T(8,128)(2,1)S(1)}, bf16[16,3584]{1,0:T(8,128)(2,1)S(1)}, u32[]{:S(2)}, u32[]{:S(2)}) collective-permute-start(bf16[16,3584]{1,0:T(8,128)(2,1)S(1)} %get-tuple-element.16), channel_id=1, source_target_pairs={{0,96},{16,112},{1,97},{17,113},{2,98},{18,114},{3,99},{19,115},{4... | collective-permute-start | bytes 344072 | tf_op jit(solution)/shard_map/ppermute | solution.py:206

commit v4 on v3

--- a/solution.py
+++ b/solution.py
@@ -148,25 +148,25 @@
     )(act, dec, after)
 
 
-def skip_product(rows, weight, start, begin, width, after):
-    tokens, span = rows.shape[0], weight.shape[1]
-
-    def kernel(rows_ref, weight_ref, after_ref, out_ref):
-        out_ref[...] = jnp.dot(
-            rows_ref[:, start : start + span], weight_ref[0, :, begin : begin + width], preferred_element_type=F32
-        ).astype(BF)
-
-    return pl.pallas_call(
-        kernel,
-        out_shape=jax.ShapeDtypeStruct((tokens, width), BF),
-        in_specs=[whole(pltpu.VMEM), whole(pltpu.VMEM), whole(pl.ANY)],
-        out_specs=whole(pltpu.VMEM),
+def skip_product(rows, weight, start, split):
+    tokens, span, width = rows.shape[0], weight.shape[1], weight.shape[2]
+
+    def kernel(rows_ref, weight_ref, first_ref, second_ref):
+        x = rows_ref[:, start : start + span]
+        first_ref[...] = jnp.dot(x, weight_ref[0, :, :split], preferred_element_type=F32).astype(BF)
+        second_ref[...] = jnp.dot(x, weight_ref[0, :, split:], preferred_element_type=F32).astype(BF)
+
+    return pl.pallas_call(
+        kernel,
+        out_shape=[jax.ShapeDtypeStruct((tokens, w), BF) for w in (split, width - split)],
+        in_specs=[whole(pltpu.VMEM)] * 2,
+        out_specs=[whole(pltpu.VMEM)] * 2,
         compiler_params=pltpu.CompilerParams(vmem_limit_bytes=VMEM_LIMIT),
         cost_estimate=pl.CostEstimate(flops=2 * tokens * span * width, bytes_accessed=(tokens + span) * width * 2, transcendentals=0),
-    )(rows, weight, after)
-
-
-PIECES = 1
+    )(rows, weight)
+
+
+SPLIT = 2304
 
 
 def per_device(chips, across, down, acts_in, targets, enc_weight, dec_weight, thresholds, skip_weight, dec_bias, owner):
@@ -189,16 +189,16 @@
     far = lax.ppermute(near, "layer", swap)
     sent = pick_rows(near, far, place, cut)
     rows = lax.all_to_all(sent, "feat", 0, 0).reshape(tokens, sent.shape[2])
-    half = depth // 2
-    skip_a = skip_product(rows, skip_weight, depth, 0, half, place)
+    half = SPLIT
+    skip_a, skip_b = skip_product(rows, skip_weight, depth, half)
     skip_a_back = lax.all_to_all(skip_a.reshape(width, shard, half), "feat", 0, 0)
 
     _, part = encode_decode(rows, enc_weight, thresholds, dec_weight, depth, skip_a)
     part, skip_a_back = lax.optimization_barrier((part, skip_a_back))
 
     back = lax.all_to_all(part.reshape(width, shard, depth), "feat", 0, 0)
-    skip_b = skip_product(rows, skip_weight, depth, half, half, back)
-    skip_b_back = lax.all_to_all(skip_b.reshape(width, shard, half), "feat", 0, 0)
+    back, skip_b = lax.optimization_barrier((back, skip_b))
+    skip_b_back = lax.all_to_all(skip_b.reshape(width, shard, depth - half), "feat", 0, 0)
     kept, given = sum_by_place(back, place, chips, skip_b)
     taken = lax.ppermute(given, "layer", swap)
     pair = (kept.astype(F32) + taken.astype(F32)).astype(BF)

time: 130 us -> 125 us (0.962)
  blocking collectives: 66.4 us -> 62.8 us
    all_to_all x1, waiting for transfers between devices: 10.6 us -> 6.27 us  [per_device(): lax.all_to_all(skip_b.reshape(width, shard, depth - half), 'feat', 0, 0)]
    all_to_all x1, blocking collectives: 31 us -> 27.4 us  [per_device(): back = lax.all_to_all(part.reshape(width, shard, depth), 'feat', 0, 0)]
    all_to_all x1, waiting for transfers between devices: 0.81 us -> 4.15 us  [per_device(): lax.all_to_all(skip_a.reshape(width, shard, half), 'feat', 0, 0)]
    pallas_call x2 -> x1, Pallas kernels: 2.95 us -> 1.86 us  [skip_product(): pl.pallas_call(kernel, out_shape=[jax.ShapeDtypeStruct((tokens, w), BF) f...]
  transfers between devices with their start and end apart: 10 -> 10, of which waited for: 5 -> 5; matrix products, arithmetic and copies ran while one was open for 2% -> 3% of each run, Pallas kernels for 11% -> 12%
where the time goes in v4:
time: 125 us; the launch traced here: 124 us
  blocking collectives  62.8 us (50%)
  waiting for transfers between devices  19.3 us (15%)
  Pallas kernels  18.9 us (15%)
  starting transfers between devices  17.9 us (14%)
  other arithmetic  3.86 us (3%)
    all_to_all x1, blocking collectives, per_device(): rows = lax.all_to_all(sent, 'feat', 0, 0).reshape(tokens, sent.shape[2])  35.4 us
    all_to_all x1, blocking collectives, per_device(): back = lax.all_to_all(part.reshape(width, shard, depth), 'feat', 0, 0)  27.4 us
    pallas_call x1, Pallas kernels, encode_decode(): pl.pallas_call(kernel, out_shape=[jax.ShapeDtypeStruct((tokens, features)...  14.5 us
    ppermute x3, waiting for transfers between devices, per_device(): lax.ppermute(acts_in[0], 'layer', [(i, i - 2 * s) for i in range(2 * s, l...  8.89 us
    ppermute x3, starting transfers between devices, per_device(): lax.ppermute(pair[s], 'layer', [(i, i + 2 * s) for i in range(layers - 2...  6.36 us
    all_to_all x1, waiting for transfers between devices, per_device(): lax.all_to_all(skip_b.reshape(width, shard, depth - half), 'feat', 0, 0)  6.27 us
    all_to_all x1, waiting for transfers between devices, per_device(): lax.all_to_all(skip_a.reshape(width, shard, half), 'feat', 0, 0)  4.15 us
    ppermute x3, starting transfers between devices, per_device(): lax.ppermute(acts_in[0], 'layer', [(i, i - 2 * s) for i in range(2 * s, l...  3.86 us
  transfers between devices with their start and end apart: 10, of which 5 were waited for; matrix products, arithmetic and copies ran while one was open for 3% of the time, Pallas kernels for 12%

profile of v4, /device:TPU:0, one launch (start us, length us, event | category | flops | bytes accessed | tf_op | source)
XLA Modules:
  0.0 124.3 jit_solution(17535237831093438513)
XLA Ops:
  0.0 1.3 %collective-permute-start = (bf16[16,3584]{1,0:T(8,128)(2,1)}, bf16[16,3584]{1,0:T(8,128)(2,1)S(1)}, u32[]{:S(2)}, u32[]{:S(2)}) collective-permute-start(bf16[16,3584]{1,0:T(8,128)(2,1)} %bitcast.35), channel_id=1, source_target_pairs={{32,0},{48,16},{64,32},{80,48},{96,64},{112,80},{33,1},{49,17},{65... | collective-permute-start | bytes 344072 | tf_op jit(solution)/shard_map/ppermute | solution.py:186
  1.3 1.3 %collective-permute-start.1 = (bf16[16,3584]{1,0:T(8,128)(2,1)}, bf16[16,3584]{1,0:T(8,128)(2,1)S(1)}, u32[]{:S(2)}, u32[]{:S(2)}) collective-permute-start(bf16[16,3584]{1,0:T(8,128)(2,1)} %bitcast.36), channel_id=1, source_target_pairs={{64,0},{80,16},{96,32},{112,48},{65,1},{81,17},{97,33},{113,49},{6... | collective-permute-start | bytes 344072 | tf_op jit(solution)/shard_map/ppermute | solution.py:186
  2.6 1.3 %collective-permute-start.2 = (bf16[16,3584]{1,0:T(8,128)(2,1)}, bf16[16,3584]{1,0:T(8,128)(2,1)S(1)}, u32[]{:S(2)}, u32[]{:S(2)}) collective-permute-start(bf16[16,3584]{1,0:T(8,128)(2,1)} %bitcast.37), channel_id=1, source_target_pairs={{96,0},{112,16},{97,1},{113,17},{98,2},{114,18},{99,3},{115,19},{1... | collective-permute-start | bytes 344072 | tf_op jit(solution)/shard_map/ppermute | solution.py:186
  3.9 3.0 %collective-permute-done = bf16[16,3584]{1,0:T(8,128)(2,1)S(1)} collective-permute-done((bf16[16,3584]{1,0:T(8,128)(2,1)}, bf16[16,3584]{1,0:T(8,128)(2,1)S(1)}, u32[]{:S(2)}, u32[]{:S(2)}) %collective-permute-start) | collective-permute-done | bytes 114720 | tf_op jit(solution)/shard_map/ppermute | solution.py:186
  6.9 3.0 %collective-permute-done.1 = bf16[16,3584]{1,0:T(8,128)(2,1)S(1)} collective-permute-done((bf16[16,3584]{1,0:T(8,128)(2,1)}, bf16[16,3584]{1,0:T(8,128)(2,1)S(1)}, u32[]{:S(2)}, u32[]{:S(2)}) %collective-permute-start.1) | collective-permute-done | bytes 114720 | tf_op jit(solution)/shard_map/ppermute | solution.py:186
  9.9 2.9 %collective-permute-done.2 = bf16[16,3584]{1,0:T(8,128)(2,1)S(1)} collective-permute-done((bf16[16,3584]{1,0:T(8,128)(2,1)}, bf16[16,3584]{1,0:T(8,128)(2,1)S(1)}, u32[]{:S(2)}, u32[]{:S(2)}) %collective-permute-start.2) | collective-permute-done | bytes 114720 | tf_op jit(solution)/shard_map/ppermute | solution.py:186
  12.8 1.0 pad_maximum_fusion.near_ref
  13.7 0.1 collective-permute-start.3
  13.8 1.1 reshape_squeeze.3
  15.0 0.7 fusion.6.place_ref
  15.8 0.0 collective-permute-done.3.far_ref
  15.8 0.8 shard_map.82
  16.6 0.0 copy-start.1
  16.7 35.4 %all_to_all.20 = bf16[16,16,3840]{2,1,0:T(8,128)(2,1)S(1)} all-to-all(bf16[16,16,3840]{2,1,0:T(8,128)(2,1)S(1)} %shard_map.82), channel_id=1, replica_groups=mesh['layer'=8,'feat'=16] {'feat'}, dimensions={0} | all-to-all | bytes 3932160 | tf_op jit(solution)/shard_map/all_to_all | solution.py:191
  52.0 0.0 copy-start
  52.0 0.0 copy-done.1
  52.0 1.9 %shard_map.83 = (bf16[256,2304]{1,0:T(8,128)(2,1)}, bf16[256,1280]{1,0:T(8,128)(2,1)}) custom-call(bf16[256,3840]{1,0:T(8,128)(2,1)S(1)} %bitcast.31, bf16[1,224,3584]{2,1,0:T(8,128)(2,1)S(1)} %copy-done.1), custom_call_target="tpu_custom_call" | custom-call | flops 411041792 | bytes 3440640 | tf_op jit(solution)/shard_map/pallas_call | solution.py:159
  53.9 0.0 copy-done
  53.9 3.7 %all-to-all-start.1 = ((bf16[16,16,2304]{2,1,0:T(8,128)(2,1)}), bf16[16,16,2304]{2,1,0:T(8,128)(2,1)S(1)}, u32[]{:S(2)}, u32[]{:S(2)}) async-start(bf16[16,16,2304]{2,1,0:T(8,128)(2,1)} %bitcast.6), calls=%async_computation.1 | async-start | bytes 2359296 | tf_op jit(solution)/shard_map/all_to_all | solution.py:194
  57.6 14.5 %shard_map.84 = (bf16[256,1536]{1,0:T(8,128)(2,1)}, bf16[256,3584]{1,0:T(8,128)(2,1)}) custom-call(bf16[256,3840]{1,0:T(8,128)(2,1)} %bitcast.32, bf16[1,3584,1536]{2,1,0:T(8,128)(2,1)} %enc_ref.1, f32[1,1536]{1,0:T(1,128)} %thr_ref.1, bf16[1,1536,3584]{2,1,0:T(8,128)(2,1)} %dec_ref.1, bf16[256,2304]{1,0:T(8,128)(2,1)} %get-tuple-element.14.after_ref), custom_call_target="tpu_custom_call" | custom-call | flops 5637144576 | bytes 22020096 | tf_op jit(solution)/shard_map/pallas_call | solution.py:106
  72.1 4.1 %all-to-all-done.1 = bf16[16,16,2304]{2,1,0:T(8,128)(2,1)S(1)} async-done(((bf16[16,16,2304]{2,1,0:T(8,128)(2,1)}), bf16[16,16,2304]{2,1,0:T(8,128)(2,1)S(1)}, u32[]{:S(2)}, u32[]{:S(2)}) %all-to-all-start.1) | async-done | bytes 1179680 | tf_op jit(solution)/shard_map/all_to_all | solution.py:194
  76.3 27.4 %all_to_all.21.parts_ref = bf16[16,16,3584]{2,1,0:T(8,128)(2,1)S(1)} all-to-all(bf16[16,16,3584]{2,1,0:T(8,128)(2,1)} %bitcast.34), channel_id=1, replica_groups=mesh['layer'=8,'feat'=16] {'feat'}, dimensions={0} | all-to-all | bytes 3670016 | tf_op jit(solution)/shard_map/all_to_all | solution.py:199
  103.7 0.0 copy-start.3
  103.7 1.7 %shard_map.85 = (bf16[4,16,3584]{2,1,0:T(8,128)(2,1)S(1)}, bf16[4,16,3584]{2,1,0:T(8,128)(2,1)S(1)}) custom-call(s32[16]{0:T(128)S(1)} %fusion.6.place_ref, bf16[16,16,3584]{2,1,0:T(8,128)(2,1)S(1)} %all_to_all.21.parts_ref, bf16[256,1280]{1,0:T(8,128)(2,1)} %get-tuple-element.19.after_ref), custom_call_target="tpu_custom_call" | custom-call | flops 917504 | bytes 2752512 | tf_op jit(solution)/shard_map/pallas_call | solution.py:65
  105.4 0.1 collective-permute-start.4
  105.5 0.0 copy-done.3
  105.6 0.2 convert_reduce_fusion
  105.7 0.0 copy-start.2
  105.7 3.8 %all-to-all-start.3 = ((bf16[16,16,1280]{2,1,0:T(8,128)(2,1)}), bf16[16,16,1280]{2,1,0:T(8,128)(2,1)S(1)}, u32[]{:S(2)}, u32[]{:S(2)}) async-start(bf16[16,16,1280]{2,1,0:T(8,128)(2,1)} %bitcast.12), calls=%async_computation.3 | async-start | bytes 1310720 | tf_op jit(solution)/shard_map/all_to_all | solution.py:201
  109.6 0.0 collective-permute-done.4
  109.6 1.1 add_convert_fusion
  110.7 1.4 %collective-permute-start.5 = (bf16[16,3584]{1,0:T(8,128)(2,1)S(1)}, bf16[16,3584]{1,0:T(8,128)(2,1)S(1)}, u32[]{:S(2)}, u32[]{:S(2)}) collective-permute-start(bf16[16,3584]{1,0:T(8,128)(2,1)S(1)} %get-tuple-element.23), channel_id=1, source_target_pairs={{0,32},{16,48},{32,64},{48,80},{64,96},{80,112},{1,33},{17,49},{33... | collective-permute-start | bytes 344072 | tf_op jit(solution)/shard_map/ppermute | solution.py:206
  112.2 3.6 %collective-permute-start.6 = (bf16[16,3584]{1,0:T(8,128)(2,1)S(1)}, bf16[16,3584]{1,0:T(8,128)(2,1)S(1)}, u32[]{:S(2)}, u32[]{:S(2)}) collective-permute-start(bf16[16,3584]{1,0:T(8,128)(2,1)S(1)} %get-tuple-element.25), channel_id=1, source_target_pairs={{0,64},{16,80},{32,96},{48,112},{1,65},{17,81},{33,97},{49,113},{2... | collective-permute-start | bytes 344072 | tf_op jit(solution)/shard_map/ppermute | solution.py:206
  115.8 1.3 %collective-permute-start.7 = (bf16[16,3584]{1,0:T(8,128)(2,1)S(1)}, bf16[16,3584]{1,0:T(8,128)(2,1)S(1)}, u32[]{:S(2)}, u32[]{:S(2)}) collective-permute-start(bf16[16,3584]{1,0:T(8,128)(2,1)S(1)} %get-tuple-element.24), channel_id=1, source_target_pairs={{0,96},{16,112},{1,97},{17,113},{2,98},{18,114},{3,99},{19,115},{4... | collective-permute-start | bytes 344072 | tf_op jit(solution)/shard_map/ppermute | solution.py:206
  117.1 6.3 %all-to-all-done.3 = bf16[16,16,1280]{2,1,0:T(8,128)(2,1)S(1)} async-done(((bf16[16,16,1280]{2,1,0:T(8,128)(2,1)}), bf16[16,16,1280]{2,1,0:T(8,128)(2,1)S(1)}, u32[]{:S(2)}, u32[]{:S(2)}) %all-to-all-start.3) | async-done | bytes 655392 | tf_op jit(solution)/shard_map/all_to_all | solution.py:201
  123.4 0.1 convert_reduce_fusion.1
  123.5 0.0 collective-permute-done.5
  123.5 0.0 collective-permute-done.6
  123.5 0.0 collective-permute-done.7
  123.5 0.0 copy-done.2
  123.5 0.7 fusion.5
  (3 shorter events, 0.1 us)
Async XLA Ops:
  0.0 6.9 %collective-permute-start = (bf16[16,3584]{1,0:T(8,128)(2,1)}, bf16[16,3584]{1,0:T(8,128)(2,1)S(1)}, u32[]{:S(2)}, u32[]{:S(2)}) collective-permute-start(bf16[16,3584]{1,0:T(8,128)(2,1)} %bitcast.35), channel_id=1, source_target_pairs={{32,0},{48,16},{64,32},{80,48},{96,64},{112,80},{33,1},{49,17},{65... | collective-permute-start | bytes 344072 | tf_op jit(solution)/shard_map/ppermute | solution.py:186
  1.3 8.6 %collective-permute-start.1 = (bf16[16,3584]{1,0:T(8,128)(2,1)}, bf16[16,3584]{1,0:T(8,128)(2,1)S(1)}, u32[]{:S(2)}, u32[]{:S(2)}) collective-permute-start(bf16[16,3584]{1,0:T(8,128)(2,1)} %bitcast.36), channel_id=1, source_target_pairs={{64,0},{80,16},{96,32},{112,48},{65,1},{81,17},{97,33},{113,49},{6... | collective-permute-start | bytes 344072 | tf_op jit(solution)/shard_map/ppermute | solution.py:186
  2.6 10.2 %collective-permute-start.2 = (bf16[16,3584]{1,0:T(8,128)(2,1)}, bf16[16,3584]{1,0:T(8,128)(2,1)S(1)}, u32[]{:S(2)}, u32[]{:S(2)}) collective-permute-start(bf16[16,3584]{1,0:T(8,128)(2,1)} %bitcast.37), channel_id=1, source_target_pairs={{96,0},{112,16},{97,1},{113,17},{98,2},{114,18},{99,3},{115,19},{1... | collective-permute-start | bytes 344072 | tf_op jit(solution)/shard_map/ppermute | solution.py:186
  13.7 2.0 %collective-permute-start.3 = (bf16[4,16,3584]{2,1,0:T(8,128)(2,1)S(1)}, bf16[4,16,3584]{2,1,0:T(8,128)(2,1)S(1)}, u32[]{:S(2)}, u32[]{:S(2)}) collective-permute-start(bf16[4,16,3584]{2,1,0:T(8,128)(2,1)S(1)} %pad_maximum_fusion.near_ref), channel_id=1, source_target_pairs={{0,16},{16,0},{32,48},{48,32},{64,80},{80,64},{96,112},{112,96},{1... | collective-permute-start | bytes 1376264 | tf_op jit(solution)/shard_map/ppermute | solution.py:189
  16.6 35.4 %copy-start.1 = (bf16[1,224,3584]{2,1,0:T(8,128)(2,1)S(1)}, bf16[1,224,3584]{2,1,0:T(8,128)(2,1)}, u32[]{:S(2)}) copy-start(bf16[1,224,3584]{2,1,0:T(8,128)(2,1)} %weight_ref.1) | copy-start | bytes 4816900
  52.0 1.9 %copy-start = (bf16[16,16,3840]{2,1,0:T(8,128)(2,1)}, bf16[16,16,3840]{2,1,0:T(8,128)(2,1)S(1)}, u32[]{:S(2)}) copy-start(bf16[16,16,3840]{2,1,0:T(8,128)(2,1)S(1)} %all_to_all.20) | copy-start | bytes 5898244
  53.9 22.4 %all-to-all-start.1 = ((bf16[16,16,2304]{2,1,0:T(8,128)(2,1)}), bf16[16,16,2304]{2,1,0:T(8,128)(2,1)S(1)}, u32[]{:S(2)}, u32[]{:S(2)}) async-start(bf16[16,16,2304]{2,1,0:T(8,128)(2,1)} %bitcast.6), calls=%async_computation.1 | async-start | bytes 2359296 | tf_op jit(solution)/shard_map/all_to_all | solution.py:194
  103.7 1.8 %copy-start.3 = (f32[1,3584]{1,0:T(1,128)S(1)}, f32[1,3584]{1,0:T(1,128)}, u32[]{:S(2)}) copy-start(f32[1,3584]{1,0:T(1,128)} %param.14) | copy-start | bytes 43012
  105.4 4.2 %collective-permute-start.4 = (bf16[4,16,3584]{2,1,0:T(8,128)(2,1)S(1)}, bf16[4,16,3584]{2,1,0:T(8,128)(2,1)}, u32[]{:S(2)}, u32[]{:S(2)}) collective-permute-start(bf16[4,16,3584]{2,1,0:T(8,128)(2,1)S(1)} %get-tuple-element.21), channel_id=1, source_target_pairs={{0,16},{16,0},{32,48},{48,32},{64,80},{80,64},{96,112},{112,96},{1... | collective-permute-start | bytes 1376264 | tf_op jit(solution)/shard_map/ppermute | solution.py:203
  105.7 17.8 %copy-start.2 = (bf16[1,16,3584]{2,1,0:T(8,128)(2,1)S(1)}, bf16[1,16,3584]{2,1,0:T(8,128)(2,1)}, u32[]{:S(2)}) copy-start(bf16[1,16,3584]{2,1,0:T(8,128)(2,1)} %param.9) | copy-start | bytes 344068
  105.7 17.6 %all-to-all-start.3 = ((bf16[16,16,1280]{2,1,0:T(8,128)(2,1)}), bf16[16,16,1280]{2,1,0:T(8,128)(2,1)S(1)}, u32[]{:S(2)}, u32[]{:S(2)}) async-start(bf16[16,16,1280]{2,1,0:T(8,128)(2,1)} %bitcast.12), calls=%async_computation.3 | async-start | bytes 1310720 | tf_op jit(solution)/shard_map/all_to_all | solution.py:201
  110.7 12.7 %collective-permute-start.5 = (bf16[16,3584]{1,0:T(8,128)(2,1)S(1)}, bf16[16,3584]{1,0:T(8,128)(2,1)S(1)}, u32[]{:S(2)}, u32[]{:S(2)}) collective-permute-start(bf16[16,3584]{1,0:T(8,128)(2,1)S(1)} %get-tuple-element.23), channel_id=1, source_target_pairs={{0,32},{16,48},{32,64},{48,80},{64,96},{80,112},{1,33},{17,49},{33... | collective-permute-start | bytes 344072 | tf_op jit(solution)/shard_map/ppermute | solution.py:206
  112.2 11.3 %collective-permute-start.6 = (bf16[16,3584]{1,0:T(8,128)(2,1)S(1)}, bf16[16,3584]{1,0:T(8,128)(2,1)S(1)}, u32[]{:S(2)}, u32[]{:S(2)}) collective-permute-start(bf16[16,3584]{1,0:T(8,128)(2,1)S(1)} %get-tuple-element.25), channel_id=1, source_target_pairs={{0,64},{16,80},{32,96},{48,112},{1,65},{17,81},{33,97},{49,113},{2... | collective-permute-start | bytes 344072 | tf_op jit(solution)/shard_map/ppermute | solution.py:206
  115.8 7.7 %collective-permute-start.7 = (bf16[16,3584]{1,0:T(8,128)(2,1)S(1)}, bf16[16,3584]{1,0:T(8,128)(2,1)S(1)}, u32[]{:S(2)}, u32[]{:S(2)}) collective-permute-start(bf16[16,3584]{1,0:T(8,128)(2,1)S(1)} %get-tuple-element.24), channel_id=1, source_target_pairs={{0,96},{16,112},{1,97},{17,113},{2,98},{18,114},{3,99},{19,115},{4... | collective-permute-start | bytes 344072 | tf_op jit(solution)/shard_map/ppermute | solution.py:206

commit v5 on v4

--- a/solution.py
+++ b/solution.py
@@ -182,12 +182,10 @@
 
     cut = acts_in[0].reshape(shard, width, span).transpose(1, 0, 2)
 
-    later = [
-        lax.ppermute(acts_in[0], "layer", [(i, i - 2 * s) for i in range(2 * s, layers)]) for s in range(1, chips)
-    ]
-    near = jnp.stack([acts_in[0], *later])
+    same_core = [[2 * x + c for x in range(chips)] for c in range(2)]
+    near = lax.all_gather(acts_in[0], "layer", axis=0, axis_index_groups=same_core)
     far = lax.ppermute(near, "layer", swap)
-    sent = pick_rows(near, far, place, cut)
+    sent = pick_rows(near, far, mine // 2 + chips * (mine % 2 != core).astype(jnp.int32), cut)
     rows = lax.all_to_all(sent, "feat", 0, 0).reshape(tokens, sent.shape[2])
     half = SPLIT
     skip_a, skip_b = skip_product(rows, skip_weight, depth, half)

time: 125 us -> 125 us (level)
  blocking collectives: 62.8 us -> 76 us
  waiting for transfers between devices: 19.3 us -> 7.14 us
    all_gather x0 -> x1, blocking collectives: none -> 13.3 us  [per_device(): lax.all_gather(acts_in[0], 'layer', axis=0, axis_index_groups=same_core)]
    ppermute x3 -> x0, waiting for transfers between devices: 8.89 us -> none  [per_device(): lax.ppermute(acts_in[0], 'layer', [(i, i - 2 * s) for i in range(2 * s, l...]
    ppermute x3 -> x0, starting transfers between devices: 3.86 us -> none  [per_device(): lax.ppermute(acts_in[0], 'layer', [(i, i - 2 * s) for i in range(2 * s, l...]
    ppermute x3, starting transfers between devices: 6.36 us -> 9.68 us  [per_device(): lax.ppermute(pair[s], 'layer', [(i, i + 2 * s) for i in range(layers - 2...]
    all_to_all x1, waiting for transfers between devices: 6.27 us -> 2.95 us  [per_device(): lax.all_to_all(skip_b.reshape(width, shard, depth - half), 'feat', 0, 0)]
  transfers between devices with their start and end apart: 10 -> 7, of which waited for: 5 -> 2; matrix products, arithmetic and copies ran while one was open for 3% -> 3% of each run, Pallas kernels for 12% -> 12%
where the time goes in v5:
time: 125 us; the launch traced here: 124 us
  blocking collectives  76 us (61%)
  Pallas kernels  18.9 us (15%)
  starting transfers between devices  17.3 us (14%)
  waiting for transfers between devices  7.14 us (6%)
  other arithmetic  2.91 us (2%)
    all_to_all x1, blocking collectives, per_device(): rows = lax.all_to_all(sent, 'feat', 0, 0).reshape(tokens, sent.shape[2])  35.3 us
    all_to_all x1, blocking collectives, per_device(): back = lax.all_to_all(part.reshape(width, shard, depth), 'feat', 0, 0)  27.4 us
    pallas_call x1, Pallas kernels, encode_decode(): pl.pallas_call(kernel, out_shape=[jax.ShapeDtypeStruct((tokens, features)...  14.5 us
    all_gather x1, blocking collectives, per_device(): lax.all_gather(acts_in[0], 'layer', axis=0, axis_index_groups=same_core)  13.3 us
    ppermute x3, starting transfers between devices, per_device(): lax.ppermute(pair[s], 'layer', [(i, i + 2 * s) for i in range(layers - 2...  9.68 us
    all_to_all x1, waiting for transfers between devices, per_device(): lax.all_to_all(skip_a.reshape(width, shard, half), 'feat', 0, 0)  4.18 us
    all_to_all x1, starting transfers between devices, per_device(): lax.all_to_all(skip_b.reshape(width, shard, depth - half), 'feat', 0, 0)  3.82 us
    all_to_all x1, starting transfers between devices, per_device(): lax.all_to_all(skip_a.reshape(width, shard, half), 'feat', 0, 0)  3.72 us
  transfers between devices with their start and end apart: 7, of which 2 were waited for; matrix products, arithmetic and copies ran while one was open for 3% of the time, Pallas kernels for 12%

profile of v5, /device:TPU:0, one launch (start us, length us, event | category | flops | bytes accessed | tf_op | source)
XLA Modules:
  0.0 123.6 jit_solution(18377075371257206597)
XLA Ops:
  0.0 13.3 %all_gather.3.near_ref = bf16[4,16,3584]{2,1,0:T(8,128)(2,1)S(1)} all-gather(bf16[1,16,3584]{2,1,0:T(8,128)(2,1)} %param.8), channel_id=1, replica_groups={{0,32,64,96},{16,48,80,112},{1,33,65,97},{17,49,81,113},{2,34,66,98},{1..., dimensions={0}, use_global_device_ids=true | all-gather | bytes 573440 | tf_op jit(solution)/shard_map/all_gather | solution.py:186
  13.3 0.0 collective-permute-start
  13.3 1.1 reshape_squeeze.3
  14.5 0.7 subtract_add_fusion
  15.2 0.0 collective-permute-done.far_ref
  15.2 0.9 shard_map.82
  16.1 0.0 copy-start.1
  16.1 35.3 %all_to_all.20 = bf16[16,16,3840]{2,1,0:T(8,128)(2,1)S(1)} all-to-all(bf16[16,16,3840]{2,1,0:T(8,128)(2,1)S(1)} %shard_map.82), channel_id=1, replica_groups=mesh['layer'=8,'feat'=16] {'feat'}, dimensions={0} | all-to-all | bytes 3932160 | tf_op jit(solution)/shard_map/all_to_all | solution.py:189
  51.4 0.0 copy-start
  51.4 0.0 copy-done.1
  51.4 1.9 %shard_map.83 = (bf16[256,2304]{1,0:T(8,128)(2,1)}, bf16[256,1280]{1,0:T(8,128)(2,1)}) custom-call(bf16[256,3840]{1,0:T(8,128)(2,1)S(1)} %bitcast.27, bf16[1,224,3584]{2,1,0:T(8,128)(2,1)S(1)} %copy-done.1), custom_call_target="tpu_custom_call" | custom-call | flops 411041792 | bytes 3440640 | tf_op jit(solution)/shard_map/pallas_call | solution.py:159
  53.3 0.0 copy-done
  53.3 3.7 %all-to-all-start.1 = ((bf16[16,16,2304]{2,1,0:T(8,128)(2,1)}), bf16[16,16,2304]{2,1,0:T(8,128)(2,1)S(1)}, u32[]{:S(2)}, u32[]{:S(2)}) async-start(bf16[16,16,2304]{2,1,0:T(8,128)(2,1)} %bitcast.2), calls=%async_computation.1 | async-start | bytes 2359296 | tf_op jit(solution)/shard_map/all_to_all | solution.py:192
  57.0 14.5 %shard_map.84 = (bf16[256,1536]{1,0:T(8,128)(2,1)}, bf16[256,3584]{1,0:T(8,128)(2,1)}) custom-call(bf16[256,3840]{1,0:T(8,128)(2,1)} %bitcast.28, bf16[1,3584,1536]{2,1,0:T(8,128)(2,1)} %enc_ref.1, f32[1,1536]{1,0:T(1,128)} %thr_ref.1, bf16[1,1536,3584]{2,1,0:T(8,128)(2,1)} %dec_ref.1, bf16[256,2304]{1,0:T(8,128)(2,1)} %get-tuple-element.14.after_ref), custom_call_target="tpu_custom_call" | custom-call | flops 5637144576 | bytes 22020096 | tf_op jit(solution)/shard_map/pallas_call | solution.py:106
  71.5 4.2 %all-to-all-done.1 = bf16[16,16,2304]{2,1,0:T(8,128)(2,1)S(1)} async-done(((bf16[16,16,2304]{2,1,0:T(8,128)(2,1)}), bf16[16,16,2304]{2,1,0:T(8,128)(2,1)S(1)}, u32[]{:S(2)}, u32[]{:S(2)}) %all-to-all-start.1) | async-done | bytes 1179680 | tf_op jit(solution)/shard_map/all_to_all | solution.py:192
  75.7 27.4 %all_to_all.21.parts_ref = bf16[16,16,3584]{2,1,0:T(8,128)(2,1)S(1)} all-to-all(bf16[16,16,3584]{2,1,0:T(8,128)(2,1)} %bitcast.30), channel_id=1, replica_groups=mesh['layer'=8,'feat'=16] {'feat'}, dimensions={0} | all-to-all | bytes 3670016 | tf_op jit(solution)/shard_map/all_to_all | solution.py:197
  103.1 0.0 copy-start.3
  103.1 1.7 %shard_map.85 = (bf16[4,16,3584]{2,1,0:T(8,128)(2,1)S(1)}, bf16[4,16,3584]{2,1,0:T(8,128)(2,1)S(1)}) custom-call(s32[16]{0:T(128)S(1)} %get-tuple-element.23.place_ref, bf16[16,16,3584]{2,1,0:T(8,128)(2,1)S(1)} %all_to_all.21.parts_ref, bf16[256,1280]{1,0:T(8,128)(2,1)} %get-tuple-element.19.after_ref), custom_call_target="tpu_custom_call" | custom-call | flops 917504 | bytes 2752512 | tf_op jit(solution)/shard_map/pallas_call | solution.py:65
  104.8 0.1 collective-permute-start.1
  104.9 0.0 copy-done.3
  104.9 0.2 convert_reduce_fusion
  105.1 0.0 copy-start.2
  105.1 3.8 %all-to-all-start.3 = ((bf16[16,16,1280]{2,1,0:T(8,128)(2,1)}), bf16[16,16,1280]{2,1,0:T(8,128)(2,1)S(1)}, u32[]{:S(2)}, u32[]{:S(2)}) async-start(bf16[16,16,1280]{2,1,0:T(8,128)(2,1)} %bitcast.8), calls=%async_computation.3 | async-start | bytes 1310720 | tf_op jit(solution)/shard_map/all_to_all | solution.py:199
  108.9 0.0 collective-permute-done.1
  109.0 1.1 add_convert_fusion
  110.1 3.7 %collective-permute-start.2 = (bf16[16,3584]{1,0:T(8,128)(2,1)S(1)}, bf16[16,3584]{1,0:T(8,128)(2,1)S(1)}, u32[]{:S(2)}, u32[]{:S(2)}) collective-permute-start(bf16[16,3584]{1,0:T(8,128)(2,1)S(1)} %get-tuple-element.26), channel_id=1, source_target_pairs={{0,32},{16,48},{32,64},{48,80},{64,96},{80,112},{1,33},{17,49},{33... | collective-permute-start | bytes 344072 | tf_op jit(solution)/shard_map/ppermute | solution.py:204
  113.8 4.7 %collective-permute-start.3 = (bf16[16,3584]{1,0:T(8,128)(2,1)S(1)}, bf16[16,3584]{1,0:T(8,128)(2,1)S(1)}, u32[]{:S(2)}, u32[]{:S(2)}) collective-permute-start(bf16[16,3584]{1,0:T(8,128)(2,1)S(1)} %get-tuple-element.28), channel_id=1, source_target_pairs={{0,64},{16,80},{32,96},{48,112},{1,65},{17,81},{33,97},{49,113},{2... | collective-permute-start | bytes 344072 | tf_op jit(solution)/shard_map/ppermute | solution.py:204
  118.5 1.3 %collective-permute-start.4 = (bf16[16,3584]{1,0:T(8,128)(2,1)S(1)}, bf16[16,3584]{1,0:T(8,128)(2,1)S(1)}, u32[]{:S(2)}, u32[]{:S(2)}) collective-permute-start(bf16[16,3584]{1,0:T(8,128)(2,1)S(1)} %get-tuple-element.27), channel_id=1, source_target_pairs={{0,96},{16,112},{1,97},{17,113},{2,98},{18,114},{3,99},{19,115},{4... | collective-permute-start | bytes 344072 | tf_op jit(solution)/shard_map/ppermute | solution.py:204
  119.8 2.9 %all-to-all-done.3 = bf16[16,16,1280]{2,1,0:T(8,128)(2,1)S(1)} async-done(((bf16[16,16,1280]{2,1,0:T(8,128)(2,1)}), bf16[16,16,1280]{2,1,0:T(8,128)(2,1)S(1)}, u32[]{:S(2)}, u32[]{:S(2)}) %all-to-all-start.3) | async-done | bytes 655392 | tf_op jit(solution)/shard_map/all_to_all | solution.py:199
  122.8 0.1 convert_reduce_fusion.1
  122.9 0.0 collective-permute-done.2
  122.9 0.0 collective-permute-done.3
  122.9 0.0 collective-permute-done.4
  122.9 0.0 copy-done.2
  122.9 0.7 fusion.5
  (4 shorter events, 0.1 us)
Async XLA Ops:
  13.3 1.9 %collective-permute-start = (bf16[4,16,3584]{2,1,0:T(8,128)(2,1)S(1)}, bf16[4,16,3584]{2,1,0:T(8,128)(2,1)S(1)}, u32[]{:S(2)}, u32[]{:S(2)}) collective-permute-start(bf16[4,16,3584]{2,1,0:T(8,128)(2,1)S(1)} %all_gather.3.near_ref), channel_id=1, source_target_pairs={{0,16},{16,0},{32,48},{48,32},{64,80},{80,64},{96,112},{112,96},{1... | collective-permute-start | bytes 1376264 | tf_op jit(solution)/shard_map/ppermute | solution.py:187
  16.1 35.3 %copy-start.1 = (bf16[1,224,3584]{2,1,0:T(8,128)(2,1)S(1)}, bf16[1,224,3584]{2,1,0:T(8,128)(2,1)}, u32[]{:S(2)}) copy-start(bf16[1,224,3584]{2,1,0:T(8,128)(2,1)} %weight_ref.1) | copy-start | bytes 4816900
  51.4 1.9 %copy-start = (bf16[16,16,3840]{2,1,0:T(8,128)(2,1)}, bf16[16,16,3840]{2,1,0:T(8,128)(2,1)S(1)}, u32[]{:S(2)}) copy-start(bf16[16,16,3840]{2,1,0:T(8,128)(2,1)S(1)} %all_to_all.20) | copy-start | bytes 5898244
  53.3 22.4 %all-to-all-start.1 = ((bf16[16,16,2304]{2,1,0:T(8,128)(2,1)}), bf16[16,16,2304]{2,1,0:T(8,128)(2,1)S(1)}, u32[]{:S(2)}, u32[]{:S(2)}) async-start(bf16[16,16,2304]{2,1,0:T(8,128)(2,1)} %bitcast.2), calls=%async_computation.1 | async-start | bytes 2359296 | tf_op jit(solution)/shard_map/all_to_all | solution.py:192
  103.1 1.8 %copy-start.3 = (f32[1,3584]{1,0:T(1,128)S(1)}, f32[1,3584]{1,0:T(1,128)}, u32[]{:S(2)}) copy-start(f32[1,3584]{1,0:T(1,128)} %param.14) | copy-start | bytes 43012
  104.8 4.2 %collective-permute-start.1 = (bf16[4,16,3584]{2,1,0:T(8,128)(2,1)S(1)}, bf16[4,16,3584]{2,1,0:T(8,128)(2,1)}, u32[]{:S(2)}, u32[]{:S(2)}) collective-permute-start(bf16[4,16,3584]{2,1,0:T(8,128)(2,1)S(1)} %get-tuple-element.21), channel_id=1, source_target_pairs={{0,16},{16,0},{32,48},{48,32},{64,80},{80,64},{96,112},{112,96},{1... | collective-permute-start | bytes 1376264 | tf_op jit(solution)/shard_map/ppermute | solution.py:201
  105.1 17.8 %copy-start.2 = (bf16[1,16,3584]{2,1,0:T(8,128)(2,1)S(1)}, bf16[1,16,3584]{2,1,0:T(8,128)(2,1)}, u32[]{:S(2)}) copy-start(bf16[1,16,3584]{2,1,0:T(8,128)(2,1)} %param.9) | copy-start | bytes 344068
  105.1 17.6 %all-to-all-start.3 = ((bf16[16,16,1280]{2,1,0:T(8,128)(2,1)}), bf16[16,16,1280]{2,1,0:T(8,128)(2,1)S(1)}, u32[]{:S(2)}, u32[]{:S(2)}) async-start(bf16[16,16,1280]{2,1,0:T(8,128)(2,1)} %bitcast.8), calls=%async_computation.3 | async-start | bytes 1310720 | tf_op jit(solution)/shard_map/all_to_all | solution.py:199
  110.1 12.7 %collective-permute-start.2 = (bf16[16,3584]{1,0:T(8,128)(2,1)S(1)}, bf16[16,3584]{1,0:T(8,128)(2,1)S(1)}, u32[]{:S(2)}, u32[]{:S(2)}) collective-permute-start(bf16[16,3584]{1,0:T(8,128)(2,1)S(1)} %get-tuple-element.26), channel_id=1, source_target_pairs={{0,32},{16,48},{32,64},{48,80},{64,96},{80,112},{1,33},{17,49},{33... | collective-permute-start | bytes 344072 | tf_op jit(solution)/shard_map/ppermute | solution.py:204
  113.8 9.1 %collective-permute-start.3 = (bf16[16,3584]{1,0:T(8,128)(2,1)S(1)}, bf16[16,3584]{1,0:T(8,128)(2,1)S(1)}, u32[]{:S(2)}, u32[]{:S(2)}) collective-permute-start(bf16[16,3584]{1,0:T(8,128)(2,1)S(1)} %get-tuple-element.28), channel_id=1, source_target_pairs={{0,64},{16,80},{32,96},{48,112},{1,65},{17,81},{33,97},{49,113},{2... | collective-permute-start | bytes 344072 | tf_op jit(solution)/shard_map/ppermute | solution.py:204
  118.5 4.4 %collective-permute-start.4 = (bf16[16,3584]{1,0:T(8,128)(2,1)S(1)}, bf16[16,3584]{1,0:T(8,128)(2,1)S(1)}, u32[]{:S(2)}, u32[]{:S(2)}) collective-permute-start(bf16[16,3584]{1,0:T(8,128)(2,1)S(1)} %get-tuple-element.27), channel_id=1, source_target_pairs={{0,96},{16,112},{1,97},{17,113},{2,98},{18,114},{3,99},{19,115},{4... | collective-permute-start | bytes 344072 | tf_op jit(solution)/shard_map/ppermute | solution.py:204

commit v6 on v5

--- a/solution.py
+++ b/solution.py
@@ -186,6 +186,7 @@
     near = lax.all_gather(acts_in[0], "layer", axis=0, axis_index_groups=same_core)
     far = lax.ppermute(near, "layer", swap)
     sent = pick_rows(near, far, mine // 2 + chips * (mine % 2 != core).astype(jnp.int32), cut)
+    sent = lax.optimization_barrier(sent)
     rows = lax.all_to_all(sent, "feat", 0, 0).reshape(tokens, sent.shape[2])
     half = SPLIT
     skip_a, skip_b = skip_product(rows, skip_weight, depth, half)

time: 125 us -> 125 us (level)
  no operation moved by 1% of the time
where the time goes in v6:
time: 125 us; the launch traced here: 124 us
  blocking collectives  76 us (61%)
  Pallas kernels  18.9 us (15%)
  starting transfers between devices  17.3 us (14%)
  waiting for transfers between devices  7.1 us (6%)
  other arithmetic  2.91 us (2%)
    all_to_all x1, blocking collectives, per_device(): rows = lax.all_to_all(sent, 'feat', 0, 0).reshape(tokens, sent.shape[2])  35.3 us
    all_to_all x1, blocking collectives, per_device(): back = lax.all_to_all(part.reshape(width, shard, depth), 'feat', 0, 0)  27.4 us
    pallas_call x1, Pallas kernels, encode_decode(): pl.pallas_call(kernel, out_shape=[jax.ShapeDtypeStruct((tokens, features)...  14.5 us
    all_gather x1, blocking collectives, per_device(): lax.all_gather(acts_in[0], 'layer', axis=0, axis_index_groups=same_core)  13.3 us
    ppermute x3, starting transfers between devices, per_device(): lax.ppermute(pair[s], 'layer', [(i, i + 2 * s) for i in range(layers - 2...  9.71 us
    all_to_all x1, waiting for transfers between devices, per_device(): lax.all_to_all(skip_a.reshape(width, shard, half), 'feat', 0, 0)  4.18 us
    all_to_all x1, starting transfers between devices, per_device(): lax.all_to_all(skip_b.reshape(width, shard, depth - half), 'feat', 0, 0)  3.82 us
    all_to_all x1, starting transfers between devices, per_device(): lax.all_to_all(skip_a.reshape(width, shard, half), 'feat', 0, 0)  3.72 us
  transfers between devices with their start and end apart: 7, of which 2 were waited for; matrix products, arithmetic and copies ran while one was open for 3% of the time, Pallas kernels for 12%

profile of v6, /device:TPU:0, one launch (start us, length us, event | category | flops | bytes accessed | tf_op | source)
XLA Modules:
  0.0 123.7 jit_solution(18377075371257206597)
XLA Ops:
  0.0 13.3 %all_gather.3.near_ref = bf16[4,16,3584]{2,1,0:T(8,128)(2,1)S(1)} all-gather(bf16[1,16,3584]{2,1,0:T(8,128)(2,1)} %param.8), channel_id=1, replica_groups={{0,32,64,96},{16,48,80,112},{1,33,65,97},{17,49,81,113},{2,34,66,98},{1..., dimensions={0}, use_global_device_ids=true | all-gather | bytes 573440 | tf_op jit(solution)/shard_map/all_gather | solution.py:186
  13.3 0.0 collective-permute-start
  13.3 1.1 reshape_squeeze.3
  14.5 0.7 subtract_add_fusion
  15.2 0.0 collective-permute-done.far_ref
  15.2 0.9 shard_map.82
  16.1 0.0 copy-start.1
  16.1 35.3 %all_to_all.20 = bf16[16,16,3840]{2,1,0:T(8,128)(2,1)S(1)} all-to-all(bf16[16,16,3840]{2,1,0:T(8,128)(2,1)S(1)} %shard_map.82), channel_id=1, replica_groups=mesh['layer'=8,'feat'=16] {'feat'}, dimensions={0} | all-to-all | bytes 3932160 | tf_op jit(solution)/shard_map/all_to_all | solution.py:190
  51.4 0.0 copy-start
  51.4 0.0 copy-done.1
  51.4 1.9 %shard_map.83 = (bf16[256,2304]{1,0:T(8,128)(2,1)}, bf16[256,1280]{1,0:T(8,128)(2,1)}) custom-call(bf16[256,3840]{1,0:T(8,128)(2,1)S(1)} %bitcast.27, bf16[1,224,3584]{2,1,0:T(8,128)(2,1)S(1)} %copy-done.1), custom_call_target="tpu_custom_call" | custom-call | flops 411041792 | bytes 3440640 | tf_op jit(solution)/shard_map/pallas_call | solution.py:159
  53.3 0.0 copy-done
  53.3 3.7 %all-to-all-start.1 = ((bf16[16,16,2304]{2,1,0:T(8,128)(2,1)}), bf16[16,16,2304]{2,1,0:T(8,128)(2,1)S(1)}, u32[]{:S(2)}, u32[]{:S(2)}) async-start(bf16[16,16,2304]{2,1,0:T(8,128)(2,1)} %bitcast.2), calls=%async_computation.1 | async-start | bytes 2359296 | tf_op jit(solution)/shard_map/all_to_all | solution.py:193
  57.0 14.5 %shard_map.84 = (bf16[256,1536]{1,0:T(8,128)(2,1)}, bf16[256,3584]{1,0:T(8,128)(2,1)}) custom-call(bf16[256,3840]{1,0:T(8,128)(2,1)} %bitcast.28, bf16[1,3584,1536]{2,1,0:T(8,128)(2,1)} %enc_ref.1, f32[1,1536]{1,0:T(1,128)} %thr_ref.1, bf16[1,1536,3584]{2,1,0:T(8,128)(2,1)} %dec_ref.1, bf16[256,2304]{1,0:T(8,128)(2,1)} %get-tuple-element.14.after_ref), custom_call_target="tpu_custom_call" | custom-call | flops 5637144576 | bytes 22020096 | tf_op jit(solution)/shard_map/pallas_call | solution.py:106
  71.5 4.2 %all-to-all-done.1 = bf16[16,16,2304]{2,1,0:T(8,128)(2,1)S(1)} async-done(((bf16[16,16,2304]{2,1,0:T(8,128)(2,1)}), bf16[16,16,2304]{2,1,0:T(8,128)(2,1)S(1)}, u32[]{:S(2)}, u32[]{:S(2)}) %all-to-all-start.1) | async-done | bytes 1179680 | tf_op jit(solution)/shard_map/all_to_all | solution.py:193
  75.7 27.4 %all_to_all.21.parts_ref = bf16[16,16,3584]{2,1,0:T(8,128)(2,1)S(1)} all-to-all(bf16[16,16,3584]{2,1,0:T(8,128)(2,1)} %bitcast.30), channel_id=1, replica_groups=mesh['layer'=8,'feat'=16] {'feat'}, dimensions={0} | all-to-all | bytes 3670016 | tf_op jit(solution)/shard_map/all_to_all | solution.py:198
  103.1 0.0 copy-start.3
  103.1 1.7 %shard_map.85 = (bf16[4,16,3584]{2,1,0:T(8,128)(2,1)S(1)}, bf16[4,16,3584]{2,1,0:T(8,128)(2,1)S(1)}) custom-call(s32[16]{0:T(128)S(1)} %get-tuple-element.23.place_ref, bf16[16,16,3584]{2,1,0:T(8,128)(2,1)S(1)} %all_to_all.21.parts_ref, bf16[256,1280]{1,0:T(8,128)(2,1)} %get-tuple-element.19.after_ref), custom_call_target="tpu_custom_call" | custom-call | flops 917504 | bytes 2752512 | tf_op jit(solution)/shard_map/pallas_call | solution.py:65
  104.8 0.1 collective-permute-start.1
  104.9 0.0 copy-done.3
  105.0 0.2 convert_reduce_fusion
  105.1 0.0 copy-start.2
  105.1 3.8 %all-to-all-start.3 = ((bf16[16,16,1280]{2,1,0:T(8,128)(2,1)}), bf16[16,16,1280]{2,1,0:T(8,128)(2,1)S(1)}, u32[]{:S(2)}, u32[]{:S(2)}) async-start(bf16[16,16,1280]{2,1,0:T(8,128)(2,1)} %bitcast.8), calls=%async_computation.3 | async-start | bytes 1310720 | tf_op jit(solution)/shard_map/all_to_all | solution.py:200
  109.0 0.0 collective-permute-done.1
  109.0 1.1 add_convert_fusion
  110.1 3.8 %collective-permute-start.2 = (bf16[16,3584]{1,0:T(8,128)(2,1)S(1)}, bf16[16,3584]{1,0:T(8,128)(2,1)S(1)}, u32[]{:S(2)}, u32[]{:S(2)}) collective-permute-start(bf16[16,3584]{1,0:T(8,128)(2,1)S(1)} %get-tuple-element.26), channel_id=1, source_target_pairs={{0,32},{16,48},{32,64},{48,80},{64,96},{80,112},{1,33},{17,49},{33... | collective-permute-start | bytes 344072 | tf_op jit(solution)/shard_map/ppermute | solution.py:205
  114.0 4.6 %collective-permute-start.3 = (bf16[16,3584]{1,0:T(8,128)(2,1)S(1)}, bf16[16,3584]{1,0:T(8,128)(2,1)S(1)}, u32[]{:S(2)}, u32[]{:S(2)}) collective-permute-start(bf16[16,3584]{1,0:T(8,128)(2,1)S(1)} %get-tuple-element.28), channel_id=1, source_target_pairs={{0,64},{16,80},{32,96},{48,112},{1,65},{17,81},{33,97},{49,113},{2... | collective-permute-start | bytes 344072 | tf_op jit(solution)/shard_map/ppermute | solution.py:205
  118.6 1.3 %collective-permute-start.4 = (bf16[16,3584]{1,0:T(8,128)(2,1)S(1)}, bf16[16,3584]{1,0:T(8,128)(2,1)S(1)}, u32[]{:S(2)}, u32[]{:S(2)}) collective-permute-start(bf16[16,3584]{1,0:T(8,128)(2,1)S(1)} %get-tuple-element.27), channel_id=1, source_target_pairs={{0,96},{16,112},{1,97},{17,113},{2,98},{18,114},{3,99},{19,115},{4... | collective-permute-start | bytes 344072 | tf_op jit(solution)/shard_map/ppermute | solution.py:205
  119.9 2.9 %all-to-all-done.3 = bf16[16,16,1280]{2,1,0:T(8,128)(2,1)S(1)} async-done(((bf16[16,16,1280]{2,1,0:T(8,128)(2,1)}), bf16[16,16,1280]{2,1,0:T(8,128)(2,1)S(1)}, u32[]{:S(2)}, u32[]{:S(2)}) %all-to-all-start.3) | async-done | bytes 655392 | tf_op jit(solution)/shard_map/all_to_all | solution.py:200
  122.8 0.1 convert_reduce_fusion.1
  122.9 0.0 collective-permute-done.2
  122.9 0.0 collective-permute-done.3
  122.9 0.0 collective-permute-done.4
  122.9 0.0 copy-done.2
  122.9 0.7 fusion.5
  (4 shorter events, 0.1 us)
Async XLA Ops:
  13.3 1.9 %collective-permute-start = (bf16[4,16,3584]{2,1,0:T(8,128)(2,1)S(1)}, bf16[4,16,3584]{2,1,0:T(8,128)(2,1)S(1)}, u32[]{:S(2)}, u32[]{:S(2)}) collective-permute-start(bf16[4,16,3584]{2,1,0:T(8,128)(2,1)S(1)} %all_gather.3.near_ref), channel_id=1, source_target_pairs={{0,16},{16,0},{32,48},{48,32},{64,80},{80,64},{96,112},{112,96},{1... | collective-permute-start | bytes 1376264 | tf_op jit(solution)/shard_map/ppermute | solution.py:187
  16.1 35.3 %copy-start.1 = (bf16[1,224,3584]{2,1,0:T(8,128)(2,1)S(1)}, bf16[1,224,3584]{2,1,0:T(8,128)(2,1)}, u32[]{:S(2)}) copy-start(bf16[1,224,3584]{2,1,0:T(8,128)(2,1)} %weight_ref.1) | copy-start | bytes 4816900
  51.4 1.9 %copy-start = (bf16[16,16,3840]{2,1,0:T(8,128)(2,1)}, bf16[16,16,3840]{2,1,0:T(8,128)(2,1)S(1)}, u32[]{:S(2)}) copy-start(bf16[16,16,3840]{2,1,0:T(8,128)(2,1)S(1)} %all_to_all.20) | copy-start | bytes 5898244
  53.3 22.4 %all-to-all-start.1 = ((bf16[16,16,2304]{2,1,0:T(8,128)(2,1)}), bf16[16,16,2304]{2,1,0:T(8,128)(2,1)S(1)}, u32[]{:S(2)}, u32[]{:S(2)}) async-start(bf16[16,16,2304]{2,1,0:T(8,128)(2,1)} %bitcast.2), calls=%async_computation.1 | async-start | bytes 2359296 | tf_op jit(solution)/shard_map/all_to_all | solution.py:193
  103.1 1.8 %copy-start.3 = (f32[1,3584]{1,0:T(1,128)S(1)}, f32[1,3584]{1,0:T(1,128)}, u32[]{:S(2)}) copy-start(f32[1,3584]{1,0:T(1,128)} %param.14) | copy-start | bytes 43012
  104.8 4.2 %collective-permute-start.1 = (bf16[4,16,3584]{2,1,0:T(8,128)(2,1)S(1)}, bf16[4,16,3584]{2,1,0:T(8,128)(2,1)}, u32[]{:S(2)}, u32[]{:S(2)}) collective-permute-start(bf16[4,16,3584]{2,1,0:T(8,128)(2,1)S(1)} %get-tuple-element.21), channel_id=1, source_target_pairs={{0,16},{16,0},{32,48},{48,32},{64,80},{80,64},{96,112},{112,96},{1... | collective-permute-start | bytes 1376264 | tf_op jit(solution)/shard_map/ppermute | solution.py:202
  105.1 17.8 %copy-start.2 = (bf16[1,16,3584]{2,1,0:T(8,128)(2,1)S(1)}, bf16[1,16,3584]{2,1,0:T(8,128)(2,1)}, u32[]{:S(2)}) copy-start(bf16[1,16,3584]{2,1,0:T(8,128)(2,1)} %param.9) | copy-start | bytes 344068
  105.1 17.6 %all-to-all-start.3 = ((bf16[16,16,1280]{2,1,0:T(8,128)(2,1)}), bf16[16,16,1280]{2,1,0:T(8,128)(2,1)S(1)}, u32[]{:S(2)}, u32[]{:S(2)}) async-start(bf16[16,16,1280]{2,1,0:T(8,128)(2,1)} %bitcast.8), calls=%async_computation.3 | async-start | bytes 1310720 | tf_op jit(solution)/shard_map/all_to_all | solution.py:200
  110.1 12.7 %collective-permute-start.2 = (bf16[16,3584]{1,0:T(8,128)(2,1)S(1)}, bf16[16,3584]{1,0:T(8,128)(2,1)S(1)}, u32[]{:S(2)}, u32[]{:S(2)}) collective-permute-start(bf16[16,3584]{1,0:T(8,128)(2,1)S(1)} %get-tuple-element.26), channel_id=1, source_target_pairs={{0,32},{16,48},{32,64},{48,80},{64,96},{80,112},{1,33},{17,49},{33... | collective-permute-start | bytes 344072 | tf_op jit(solution)/shard_map/ppermute | solution.py:205
  114.0 8.9 %collective-permute-start.3 = (bf16[16,3584]{1,0:T(8,128)(2,1)S(1)}, bf16[16,3584]{1,0:T(8,128)(2,1)S(1)}, u32[]{:S(2)}, u32[]{:S(2)}) collective-permute-start(bf16[16,3584]{1,0:T(8,128)(2,1)S(1)} %get-tuple-element.28), channel_id=1, source_target_pairs={{0,64},{16,80},{32,96},{48,112},{1,65},{17,81},{33,97},{49,113},{2... | collective-permute-start | bytes 344072 | tf_op jit(solution)/shard_map/ppermute | solution.py:205
  118.6 4.3 %collective-permute-start.4 = (bf16[16,3584]{1,0:T(8,128)(2,1)S(1)}, bf16[16,3584]{1,0:T(8,128)(2,1)S(1)}, u32[]{:S(2)}, u32[]{:S(2)}) collective-permute-start(bf16[16,3584]{1,0:T(8,128)(2,1)S(1)} %get-tuple-element.27), channel_id=1, source_target_pairs={{0,96},{16,112},{1,97},{17,113},{2,98},{18,114},{3,99},{19,115},{4... | collective-permute-start | bytes 344072 | tf_op jit(solution)/shard_map/ppermute | solution.py:205
